TPU v7x, 32 devices: a whole 2x2x4 slice. The times are simulated.
32 devices in a mesh: day: 2 (over y), tm: 4 (over z), sta: 4 (over x, core).
Axes of the slice: x: 2, y: 2, z: 4, core: 2. Of those that a mesh axis runs over, the one named last changes fastest.
Arguments:
- traces: bfloat16 [2048, 24576], P('sta', ('day', 'tm')), parts along dimension 1, may hold values from -12 to 12
- offsets: int32 [24], P(('day', 'tm')), parts along dimension 0, may hold values from 0 to 3072, as said below
- pair_first: int32 [2048], P('sta'), may hold values from 0 to 511
- pair_slot: int32 [2048], P('sta'), may hold values from 0 to 127, as said below
- send_rows: int32 [4, 128], P('sta'), may hold values from 0 to 511, as said below
Outputs:
- correlations: float32 [2048, 2048], P(('day', 'tm'), 'sta'), parts along dimension 0
There are 2 independent parts, one for each index of `day`. A program takes and returns all parts, laid end to end along the dimension named above; an argument that names none is the same for every part. Nothing has to cross between parts.
Inputs may be any that keep to these rules, and one draw needn't show every extreme that they name: offsets[t * 3 + w] lies between w * 1024 and (w + 1) * 1024. For a pair owned by group g whose src = pair_slot // 32 lies two or more groups from g around the cycle of 4 groups (neither g - 1, g nor g + 1 modulo 4), pair_slot mod 32 is below 8. The 32 entries send_rows[s, g * 32 .. (g + 1) * 32 - 1] are distinct.
All inputs are finite; a program needn't handle non-finite values.
Results may differ from a plain program's by a relative error of at most 0.0039.
Values may be sent and summed in bfloat16 or wider, within the bound.
A program may use at most 64 MiB of HBM per device.

v0:
```python
import math

import jax
import jax.numpy as jnp
from jax import lax
from jax.sharding import PartitionSpec as P

WIN = 2048
NF = 512
NL = 1024


FLOOR = 0.1


def shifted(block, axis, distance):
    devices = range(lax.axis_size(axis))
    route = [(i - distance, i) for i in devices if i - distance in devices]
    return lax.ppermute(block, axis, route)


def taper_table(length):
    sample_index = jnp.arange(length, dtype=jnp.float32)
    return 0.5 - 0.5 * jnp.cos(2.0 * math.pi * sample_index / length)


def dft_table(length, bin_count):
    sample_index = jnp.arange(length, dtype=jnp.int32)[:, None]
    bin_index = jnp.arange(bin_count, dtype=jnp.int32)[None, :] + 1
    angles = (sample_index * bin_index % length).astype(jnp.float32) * (2.0 * math.pi / length)
    return jnp.concatenate([jnp.cos(angles), -jnp.sin(angles)], axis=1).astype(jnp.bfloat16)


def lag_table(lag_count, length, bin_count):
    lag_shift = jnp.arange(lag_count, dtype=jnp.int32)[:, None] - lag_count // 2
    bin_index = jnp.arange(bin_count, dtype=jnp.int32)[None, :] + 1
    angles = (lag_shift * bin_index % length).astype(jnp.float32) * (2.0 * math.pi / length)
    return jnp.concatenate([jnp.cos(angles), -jnp.sin(angles)], axis=1)


def segments(block_data, starts, length):

    def take_one(start_at):
        return lax.dynamic_slice_in_dim(block_data, start_at, length, axis=1)

    pieces = jax.vmap(take_one)(starts)
    values = pieces.astype(jnp.float32)
    centred = values - jnp.mean(values, axis=2, keepdims=True)
    return (centred * taper_table(length)).astype(jnp.bfloat16)


def whiten(spectrum, bin_count):
    real_part = spectrum[..., :bin_count]
    imag_part = spectrum[..., bin_count:]
    amplitude = jnp.sqrt(real_part * real_part + imag_part * imag_part + 1e-06)
    padded = jnp.pad(amplitude, [(0, 0)] * (amplitude.ndim - 1) + [(2, 2)])
    smooth = (
        padded[..., 0:bin_count]
        + padded[..., 1 : bin_count + 1]
        + padded[..., 2 : bin_count + 2]
        + padded[..., 3 : bin_count + 3]
        + padded[..., 4 : bin_count + 4]
    ) / 5.0
    inverse = 1.0 / jnp.maximum(smooth, FLOOR)
    return (spectrum * jnp.concatenate([inverse, inverse], axis=-1)).astype(jnp.bfloat16)


def cross_terms(first_spec, second_spec, bin_count):
    first_real = first_spec[..., :bin_count].astype(jnp.float32)
    first_imag = first_spec[..., bin_count:].astype(jnp.float32)
    second_real = second_spec[..., :bin_count].astype(jnp.float32)
    second_imag = second_spec[..., bin_count:].astype(jnp.float32)
    return jnp.concatenate(
        [
            first_real * second_real + first_imag * second_imag,
            first_imag * second_real - first_real * second_imag,
        ],
        axis=-1,
    )


def on_device(traces, offsets, pair_first, pair_slot, send_rows):
    stations = traces.shape[0]
    windows = offsets.shape[0]
    time_devices = lax.axis_size("tm")
    next_rim = shifted(traces[:, :WIN], "tm", -1)
    block_data = jnp.concatenate([traces, next_rim], axis=1)
    segment = segments(block_data, offsets, WIN)
    spectrum = jnp.dot(
        segment.reshape(windows * stations, WIN),
        dft_table(WIN, NF),
        preferred_element_type=jnp.float32,
    ) * (1.0 / math.sqrt(WIN))
    whitened = whiten(spectrum.reshape(windows, stations, 2 * NF), NF)
    row_list = send_rows[0]
    outgoing = jnp.take(whitened, row_list, axis=1)
    incoming = lax.all_to_all(outgoing, "sta", split_axis=1, concat_axis=1, tiled=True)

    def add_window(window, running):
        first_spec = jnp.take(whitened[window], pair_first, axis=0)
        second_spec = jnp.take(incoming[window], pair_slot, axis=0)
        return running + cross_terms(first_spec, second_spec, NF)

    cross_sum = lax.fori_loop(
        0, windows, add_window, jnp.zeros((pair_first.shape[0], 2 * NF), jnp.float32)
    )
    lag_rows = lag_table(NL, WIN, NF)
    scaling = 1.0 / math.sqrt(NF * windows * time_devices)
    stacked = lax.psum_scatter(
        lax.dot_general(
            lag_rows,
            cross_sum,
            (((1,), (1,)), ((), ())),
            precision=lax.Precision.HIGHEST,
            preferred_element_type=jnp.float32,
        ),
        "tm",
        scatter_dimension=0,
        tiled=True,
    )
    return stacked * scaling


def solution(mesh):
    in_specs = (P("sta", ("day", "tm")), P(("day", "tm")), P("sta"), P("sta"), P("sta", None))
    out_specs = P(("day", "tm"), "sta")
    return jax.shard_map(
        on_device, mesh=mesh, in_specs=in_specs, out_specs=out_specs, check_vma=False
    )
```

profile of v0, /device:TPU:0, one launch (start us, length us, event | category | flops | bytes accessed | tf_op | source)
XLA Modules:
  0.0 256.7 jit_solution(7347927885232624078)
XLA Ops:
  6.5 3.3 %slice.50 = bf16[512,2048]{1,0:T(8,128)(2,1)} slice(bf16[512,3072]{1,0:T(8,128)(2,1)} %param.7), slice={[0:512], [0:2048]} | slice | bytes 4194304 | tf_op jit(solution)/shard_map/slice | solution.py:86
  9.9 1.3 collective-permute-start
  11.2 0.0 copy-done.7
  11.2 0.0 copy-done.8
  11.2 0.1 multiply_subtract_fusion
  11.3 18.3 %cosine_convert_fusion = (bf16[2048,512]{1,0:T(8,128)(2,1)}, bf16[2048,512]{1,0:T(8,128)(2,1)}) fusion(s32[512]{0:T(512)S(1)} %iota_add_fusion.1), kind=kLoop, calls=%fused_computation.61 | loop fusion | flops 17825792 | bytes 4196352 | tf_op jit(solution)/shard_map/convert.1
  29.6 31.1 %collective-permute-done = bf16[512,2048]{1,0:T(8,128)(2,1)} collective-permute-done((bf16[512,2048]{1,0:T(8,128)(2,1)}, bf16[512,2048]{1,0:T(8,128)(2,1)}, u32[]{:S(2)}, u32[]{:S(2)}) %collective-permute-start) | collective-permute-done | bytes 2097184 | tf_op jit(solution)/shard_map/ppermute | solution.py:19
  60.7 0.0 copy-done.2
  60.7 4.3 %pad_maximum_fusion = bf16[512,5120]{1,0:T(8,128)(2,1)} fusion(bf16[512,2048]{1,0:T(8,128)(2,1)} %collective-permute-done, bf16[512,3072]{1,0:T(8,128)(2,1)S(1)} %copy-done.2), kind=kLoop, calls=%fused_computation.32 | loop fusion | flops 10485760 | bytes 10485760 | tf_op jit(solution)/shard_map/concatenate | solution.py:87
  65.0 16.4 %while.15 = (s32[]{:T(128)}, bf16[512,5120]{1,0:T(8,128)(2,1)}, s32[3,2]{0,1:T(2,128)S(1)}, bf16[3,512,2048]{2,1,0:T(8,128)(2,1)}, s32[]{:T(128)}) while((s32[]{:T(128)}, bf16[512,5120]{1,0:T(8,128)(2,1)}, s32[3,2]{0,1:T(2,128)S(1)}, bf16[3,512,2048]{2,1,0:T(8,128)(2,1)}, s32[]{:T(128)}) %tuple.52), condition=%wide.while_cond, body=%wide.while_body.sunk | while | flops 2 | bytes 4195417 | solution.py:44
  65.0 0.1 constant_dynamic-slice_fusion.2
  65.1 0.5 slice.133
  65.6 4.9 %bitcast_dynamic-update-slice_fusion.2 = bf16[3,512,2048]{2,1,0:T(8,128)(2,1)} fusion(bf16[3,512,2048]{2,1,0:T(8,128)(2,1)} %get-tuple-element.256, s32[]{:T(128)} %get-tuple-element.253, bf16[512,5120]{1,0:T(8,128)(2,1)} %get-tuple-element.259, s32[]{:T(128)} %bitcast.39), kind=kLoop, calls=%fused_computation.3.clone.1 | loop fusion | bytes 4195328 | tf_op jit(solution)/shard_map/vmap()/gather
  70.5 0.1 constant_dynamic-slice_fusion.2
  70.6 0.5 slice.133
  71.1 4.9 %bitcast_dynamic-update-slice_fusion.2 = bf16[3,512,2048]{2,1,0:T(8,128)(2,1)} fusion(bf16[3,512,2048]{2,1,0:T(8,128)(2,1)} %get-tuple-element.256, s32[]{:T(128)} %get-tuple-element.253, bf16[512,5120]{1,0:T(8,128)(2,1)} %get-tuple-element.259, s32[]{:T(128)} %bitcast.39), kind=kLoop, calls=%fused_computation.3.clone.1 | loop fusion | bytes 4195328 | tf_op jit(solution)/shard_map/vmap()/gather
  76.0 0.1 constant_dynamic-slice_fusion.2
  76.0 0.5 slice.133
  76.6 4.9 %bitcast_dynamic-update-slice_fusion.2 = bf16[3,512,2048]{2,1,0:T(8,128)(2,1)} fusion(bf16[3,512,2048]{2,1,0:T(8,128)(2,1)} %get-tuple-element.256, s32[]{:T(128)} %get-tuple-element.253, bf16[512,5120]{1,0:T(8,128)(2,1)} %get-tuple-element.259, s32[]{:T(128)} %bitcast.39), kind=kLoop, calls=%fused_computation.3.clone.1 | loop fusion | bytes 4195328 | tf_op jit(solution)/shard_map/vmap()/gather
  81.4 3.7 %convert_reduce_fusion = f32[3,512]{1,0:T(4,128)S(1)} fusion(bf16[3,512,2048]{2,1,0:T(8,128)(2,1)} %get-tuple-element.122), kind=kLoop, calls=%fused_computation.68 | loop fusion | flops 6289920 | bytes 6297600 | tf_op jit(solution)/shard_map/reduce_sum | solution.py:48
  85.2 4.4 %fusion.3 = bf16[1536,2048]{1,0:T(8,128)(2,1)S(1)} fusion(f32[2048]{0:T(1024)S(1)} %multiply_subtract_fusion, f32[1536]{0:T(1024)S(1)} %div.28, bf16[3,512,2048]{2,1,0:T(8,128)(2,1)} %get-tuple-element.122), kind=kLoop, calls=%fused_computation.26 | loop fusion | flops 12582912 | bytes 12597248 | tf_op jit(solution)/shard_map/convert_element_type | solution.py:49
  89.6 9.0 %convolution_multiply_fusion = f32[1536,1024]{1,0:T(8,128)} fusion(bf16[1536,2048]{1,0:T(8,128)(2,1)S(1)} %fusion.3, bf16[2048,512]{1,0:T(8,128)(2,1)S(1)} %copy-done.4, bf16[2048,512]{1,0:T(8,128)(2,1)S(1)} %copy-done.3), kind=kOutput, calls=%fused_computation.37 | convolution fusion | flops 6452412416 | bytes 16777216 | tf_op jit(solution)/shard_map/dot_general | solution.py:89
  98.6 7.1 %copy.8 = f32[3,512,1024]{2,0,1:T(4,128)S(1)} copy(f32[3,512,1024]{2,1,0:T(8,128)} %bitcast.46) | data formatting | bytes 12582912 | tf_op jit(solution)/shard_map/reshape | solution.py:94
  105.7 4.4 %fusion.17 = f32[3,512,512]{2,0,1:T(4,128)} fusion(f32[3,512,1024]{2,0,1:T(4,128)S(1)} %copy.8), kind=kLoop, calls=%fused_computation.51 | loop fusion | flops 3145728 | bytes 9437184 | tf_op jit(solution)/shard_map/sqrt | solution.py:55
  110.1 16.7 %fusion.11 = f32[3,512,512]{2,0,1:T(4,128)S(1)} fusion(f32[3,512,512]{2,0,1:T(4,128)} %fusion.17), kind=kLoop, calls=%fused_computation.44 | loop fusion | flops 5505024 | bytes 6291456 | tf_op jit(solution)/shard_map/div | solution.py:64
  126.8 0.0 copy-done
  126.8 12.6 %fusion.4 = bf16[3,512,1024]{2,0,1:T(4,128)(2,1)} fusion(f32[3,512,512]{2,0,1:T(4,128)S(1)} %fusion.11, f32[3,512,1024]{2,1,0:T(8,128)S(1)} %bitcast.47), kind=kLoop, calls=%fused_computation.28 | loop fusion | flops 4718592 | bytes 12582912 | tf_op jit(solution)/shard_map/convert_element_type | solution.py:65
  139.5 3.6 %gather_fusion.2 = bf16[128,3,1024]{2,1,0:T(4,128)(2,1)S(1)} fusion(bf16[3,512,1024]{2,0,1:T(4,128)(2,1)} %fusion.4, s32[1024]{0:T(1024)S(1)} %pad_clamp_fusion.2), kind=kCustom, calls=%fused_computation.2 | custom fusion | bytes 1573376 | tf_op jit(solution)/shard_map/jit(_take)/gather | solution.py:96
  143.1 1.5 select_bitcast_fusion
  144.7 3.5 %all-to-all-start = ((bf16[3,128,1024]{2,0,1:T(4,128)(2,1)}), bf16[3,128,1024]{2,0,1:T(4,128)(2,1)S(1)}, u32[]{:S(2)}, u32[]{:S(2)}) async-start(bf16[3,128,1024]{2,0,1:T(4,128)(2,1)} %select_bitcast_fusion), calls=%async_computation | async-start | bytes 2097152 | tf_op jit(solution)/shard_map/all_to_all | solution.py:97
  148.2 0.0 reduce-scatter.2.cloned.1.call-start
  148.3 9.8 %fusion.31 = (f32[1024,512]{1,0:T(8,128)}, f32[1024,512]{1,0:T(8,128)}) fusion(s32[512]{0:T(512)S(1)} %iota_add_fusion.1, s32[1024]{0:T(1024)S(1)} %iota_add_fusion), kind=kLoop, calls=%fused_computation.76 | loop fusion | flops 7864320 | bytes 4200448 | tf_op jit(solution)/shard_map/cos | solution.py:38
  158.1 2.9 %copy.9 = bf16[3,512,1024]{2,1,0:T(8,128)(2,1)} copy(bf16[3,512,1024]{2,0,1:T(4,128)(2,1)S(1)} %copy-done.1) | data formatting | bytes 6291456
  161.0 1.7 all-to-all-done
  162.6 1.2 copy.10
  163.8 30.4 %while.16 = (s32[]{:T(128)}, f32[512,1024]{1,0:T(8,128)}, s32[512]{0:T(512)S(1)}, bf16[3,512,1024]{2,1,0:T(8,128)(2,1)}, s32[512]{0:T(512)S(1)}, /*index=5*/bf16[3,128,1024]{2,1,0:T(8,128)(2,1)}, s32[]{:T(128)}, s32[]{:T(128)}) while((s32[]{:T(128)}, f32[512,1024]{1,0:T(8,128)}, s32[512]{0:T(512)S(1)}, ...), condition=%wide.region_2.3_spmd.clone, body=%wide.region_1.2_spmd.clone.sunk | while | flops 5254147 | bytes 21526632 | solution.py:104
  163.8 1.3 dynamic-slice_bitcast_fusion.5
  165.2 2.1 gather_fusion.1
  167.2 0.2 broadcast_select_fusion.5
  167.4 1.0 dynamic-slice_bitcast_fusion.4
  168.4 2.1 gather_fusion
  170.5 0.2 broadcast_select_fusion.4
  170.6 0.3 fusion.39
  171.0 1.9 maximum_add_fusion.2
  172.9 1.3 dynamic-slice_bitcast_fusion.5
  174.2 2.1 gather_fusion.1
  176.3 0.2 broadcast_select_fusion.5
  176.5 1.0 dynamic-slice_bitcast_fusion.4
  177.5 2.1 gather_fusion
  179.5 0.2 broadcast_select_fusion.4
  179.7 0.3 fusion.39
  180.1 3.5 %maximum_add_fusion.2 = f32[512,1024]{1,0:T(8,128)} fusion(f32[512,512]{1,0:T(8,128)S(1)} %get-tuple-element.246, f32[512,512]{1,0:T(8,128)S(1)} %get-tuple-element.247, f32[512,1024]{1,0:T(8,128)} %get-tuple-element.272, pred[]{:T(512)S(6)} %compare.9), kind=kLoop, calls=%fused_computation.5.clone.1 | loop fusion | flops 1572864 | bytes 6291457 | tf_op jit(solution)/shard_map/while/body/eval_jaxpr/add | solution.py:102
  183.6 1.3 dynamic-slice_bitcast_fusion.5
  184.9 2.1 gather_fusion.1
  187.0 0.2 broadcast_select_fusion.5
  187.1 1.0 dynamic-slice_bitcast_fusion.4
  188.1 2.1 gather_fusion
  190.2 0.2 broadcast_select_fusion.4
  190.4 0.3 fusion.39
  190.7 3.5 %maximum_add_fusion.2 = f32[512,1024]{1,0:T(8,128)} fusion(f32[512,512]{1,0:T(8,128)S(1)} %get-tuple-element.246, f32[512,512]{1,0:T(8,128)S(1)} %get-tuple-element.247, f32[512,1024]{1,0:T(8,128)} %get-tuple-element.272, pred[]{:T(512)S(6)} %compare.9), kind=kLoop, calls=%fused_computation.5.clone.1 | loop fusion | flops 1572864 | bytes 6291457 | tf_op jit(solution)/shard_map/while/body/eval_jaxpr/add | solution.py:102
  194.2 10.3 %fusion.18 = f32[1024,512]{1,0:T(8,128)} fusion(f32[512,1024]{1,0:T(8,128)} %get-tuple-element.114, f32[1024,512]{1,0:T(8,128)} %get-tuple-element.175, f32[1024,512]{1,0:T(8,128)} %get-tuple-element.174), kind=kOutput, calls=%fused_computation.53 | convolution fusion | flops 6443499520 | bytes 8388608 | tf_op jit(solution)/shard_map/dot_general | solution.py:110
  204.5 0.0 reduce-scatter.2.cloned.1.call-update
  204.5 43.4 %reduce-scatter.2.cloned.1.call-done = f32[256,512]{1,0:T(8,128)} async-done(((f32[1024,512]{1,0:T(8,128)}), f32[256,512]{1,0:T(8,128)}) %reduce-scatter.2.cloned.1.call-update) | async-done | bytes 524304 | tf_op jit(solution)/shard_map/reduce_scatter | solution.py:109
  248.0 1.9 broadcast_multiply_fusion
  (40 shorter events, 0.2 us)
Async XLA Ops:
  6.5 54.2 %copy-start.2 = (bf16[512,3072]{1,0:T(8,128)(2,1)S(1)}, bf16[512,3072]{1,0:T(8,128)(2,1)}, u32[]{:S(2)}) copy-start(bf16[512,3072]{1,0:T(8,128)(2,1)} %param.7) | copy-start | bytes 9437188
  6.5 4.6 %copy-start.7 = (s32[3]{0:T(128)S(1)}, s32[3]{0:T(128)}, u32[]{:S(2)}) copy-start(s32[3]{0:T(128)} %param.8) | copy-start | bytes 40
  6.5 4.7 %copy-start.8 = (s32[1,128]{1,0:T(1,128)S(1)}, s32[1,128]{1,0:T(1,128)}, u32[]{:S(2)}) copy-start(s32[1,128]{1,0:T(1,128)} %param.11) | copy-start | bytes 1540
  9.9 50.9 %collective-permute-start = (bf16[512,2048]{1,0:T(8,128)(2,1)}, bf16[512,2048]{1,0:T(8,128)(2,1)}, u32[]{:S(2)}, u32[]{:S(2)}) collective-permute-start(bf16[512,2048]{1,0:T(8,128)(2,1)} %slice.50), channel_id=1, source_target_pairs={{4,0},{8,4},{12,8},{5,1},{9,5},{13,9},{6,2},{10,6},{14,10},{7,3},{... | collective-permute-start | bytes 6291464 | tf_op jit(solution)/shard_map/ppermute | solution.py:19
  85.1 4.5 %copy-start.3 = (bf16[2048,512]{1,0:T(8,128)(2,1)S(1)}, bf16[2048,512]{1,0:T(8,128)(2,1)}, u32[]{:S(2)}) copy-start(bf16[2048,512]{1,0:T(8,128)(2,1)} %get-tuple-element.176) | copy-start | bytes 6291460
  85.2 4.5 %copy-start.4 = (bf16[2048,512]{1,0:T(8,128)(2,1)S(1)}, bf16[2048,512]{1,0:T(8,128)(2,1)}, u32[]{:S(2)}) copy-start(bf16[2048,512]{1,0:T(8,128)(2,1)} %get-tuple-element.177) | copy-start | bytes 6291460
  110.1 16.7 %copy-start = (f32[1536,1024]{1,0:T(8,128)S(1)}, f32[1536,1024]{1,0:T(8,128)}, u32[]{:S(2)}) copy-start(f32[1536,1024]{1,0:T(8,128)} %convolution_multiply_fusion) | copy-start | bytes 18874372
  144.7 18.0 %all-to-all-start = ((bf16[3,128,1024]{2,0,1:T(4,128)(2,1)}), bf16[3,128,1024]{2,0,1:T(4,128)(2,1)S(1)}, u32[]{:S(2)}, u32[]{:S(2)}) async-start(bf16[3,128,1024]{2,0,1:T(4,128)(2,1)} %select_bitcast_fusion), calls=%async_computation | async-start | bytes 2097152 | tf_op jit(solution)/shard_map/all_to_all | solution.py:97
  148.2 99.8 %reduce-scatter.2.cloned.1.call-start = ((), (), s32[]{:S(2)}) async-start(), calls=%async_computation.2 | async-start | bytes 2621440 | tf_op jit(solution)/shard_map/reduce_scatter | solution.py:109
  148.2 9.8 %copy-start.1 = (bf16[3,512,1024]{2,0,1:T(4,128)(2,1)S(1)}, bf16[3,512,1024]{2,0,1:T(4,128)(2,1)}, u32[]{:S(2)}) copy-start(bf16[3,512,1024]{2,0,1:T(4,128)(2,1)} %fusion.4) | copy-start | bytes 9437188
  158.1 5.8 %copy-start.5 = (s32[512]{0:T(512)S(1)}, s32[512]{0:T(512)}, u32[]{:S(2)}) copy-start(s32[512]{0:T(512)} %param.9) | copy-start | bytes 6148
  158.1 5.8 %copy-start.6 = (s32[512]{0:T(512)S(1)}, s32[512]{0:T(512)}, u32[]{:S(2)}) copy-start(s32[512]{0:T(512)} %param.10) | copy-start | bytes 6148
Sparse Core Ops, SparseCore 0:
  204.6 43.2 reduce-scatter.1
where the time goes:
time: 258 us; the launch traced here: 257 us
  other arithmetic  88.7 us (34%)
  waiting for transfers between devices  76.3 us (30%)
  local copies, waits for them, and re-layouts  53.8 us (21%)
  matrix products  19.3 us (7%)
  between operations  13.6 us (5%)
  starting transfers between devices  4.84 us (2%)
    reduce_scatter x1, waiting for transfers between devices, on_device(): lax.psum_scatter(lax.dot_general(lag_rows, cross_sum, (((1,), (1,)), ((),...  43.4 us
    ppermute x1, waiting for transfers between devices, shifted(): return lax.ppermute(block, axis, route)  31.1 us
    another operation x1, other arithmetic  18.3 us
    div x1, other arithmetic, whiten(): inverse = 1.0 / jnp.maximum(smooth, FLOOR)  16.7 us
    gather x9, local copies, waits for them, and re-layouts  16.4 us
    convert_element_type x1, other arithmetic, whiten(): (spectrum * jnp.concatenate([inverse, inverse], axis=-1)).astype(jnp.bflo...  12.6 us
    dot_general x1, matrix products, on_device(): lax.dot_general(lag_rows, cross_sum, (((1,), (1,)), ((), ())), precision=...  10.3 us
    cos x1, other arithmetic, lag_table(): return jnp.concatenate([jnp.cos(angles), -jnp.sin(angles)], axis=1)  9.78 us
  transfers between devices with their start and end apart: 3, of which 3 were waited for; matrix products, arithmetic and copies ran while one was open for 12% of the time, Pallas kernels for 0%

commit v1 on v0

v1 whole, which is shorter than its diff:
```python
import functools
import math

import jax
import jax.numpy as jnp
import numpy as np
from jax import lax
from jax.experimental import pallas as pl
from jax.experimental.pallas import tpu as pltpu
from jax.sharding import PartitionSpec as P

WIN = 2048
NF = 512
NL = 1024
STEP = 1024
TB = 3072
CAP = 32
FAR_ROWS = 16
FLOOR = 0.1
CHUNKS = 4
PIECES = 2
BLK = 128
ROWS = 16
MESH = pl.DeviceIdType.MESH


def taper_table():
    n = np.arange(WIN, dtype=np.float64)
    return (0.5 - 0.5 * np.cos(2.0 * np.pi * n / WIN)).astype(np.float32)[None, :]


def dft_table():
    n = np.arange(WIN)[:, None]
    k = np.arange(NF)[None, :] + 1
    angle = (n * k % WIN) * (2.0 * np.pi / WIN)
    return np.concatenate([np.cos(angle), -np.sin(angle)], axis=1).astype(jnp.bfloat16)


def lag_table():
    t = np.arange(NL)[:, None] - NL // 2
    k = np.arange(NF)[None, :] + 1
    angle = (t * k % WIN) * (2.0 * np.pi / WIN)
    return np.concatenate([np.cos(angle), -np.sin(angle)], axis=1).astype(jnp.bfloat16)


def shifted(blocks, jitter):
    quotient = jitter // BLK
    rest = jitter % BLK
    for bit, count in ((8, 24), (4, 20), (2, 18), (1, 17)):
        on = (quotient // bit) % 2 == 1
        blocks = [
            jnp.where(on, blocks[i + bit], blocks[i]) if i + bit < len(blocks) else blocks[i]
            for i in range(count)
        ]
    turn = (BLK - rest) % BLK
    rolled = [pltpu.roll(b, turn, 1) for b in blocks]
    lane = lax.broadcasted_iota(jnp.int32, blocks[0].shape, 1)
    keep = lane < BLK - rest
    return [jnp.where(keep, rolled[i], rolled[i + 1]) for i in range(WIN // BLK)]


def write_segment(blocks, jitter, taper, seg, row):
    values = shifted(blocks, jitter)
    total = values[0]
    for v in values[1:]:
        total = total + v
    mean = jnp.sum(total, axis=1, keepdims=True) * (1.0 / WIN)
    for i, v in enumerate(values):
        columns = slice(i * BLK, (i + 1) * BLK)
        seg[pl.ds(row, ROWS), columns] = ((v - mean) * taper[:, columns]).astype(jnp.bfloat16)


def load_blocks(ref, row, first, count):
    return [
        ref[pl.ds(row, ROWS), i * BLK : (i + 1) * BLK].astype(jnp.float32)
        for i in range(first, first + count)
    ]


def whiten_rows(spec, row):
    re = spec[pl.ds(row, ROWS), :NF]
    im = spec[pl.ds(row, ROWS), NF:]
    amplitude = jnp.sqrt(re * re + im * im + 1e-06)
    wide = jnp.concatenate([amplitude, jnp.zeros((ROWS, BLK), jnp.float32)], axis=1)
    width = NF + BLK
    pair = wide + pltpu.roll(wide, 1, 1)
    five = wide + pltpu.roll(pair, 1, 1) + pltpu.roll(pair, width - 2, 1)
    inverse = 1.0 / jnp.maximum(five[:, :NF] * (1.0 / 5.0), FLOOR)
    return (re * inverse).astype(jnp.bfloat16), (im * inverse).astype(jnp.bfloat16)


def kernel(
    n_tm, n_sta,
    offsets, pair_first, pair_slot, send_rows, taper, traces, table_hbm, lag_hbm,
    out,
    own, rim_prev, rim_next, table, lags, seg, spec, white, outgoing, incoming,
    pick_first, pick_second, pick_send, first_rows, cross_sum, cross,
    up_send, up_recv, down_send, down_recv, offset_send, offset_recv,
    local_sem, rim_send_sem, rim_recv_sem, offset_sem, swap_send_sem, swap_recv_sem,
    up_send_sem, up_recv_sem, down_send_sem, down_recv_sem,
):
    stations = own.shape[0]
    pairs = out.shape[1]
    lag_rows = out.shape[0]
    slots = n_sta * CAP
    chunk = stations // CHUNKS
    tm = lax.axis_index("tm")
    me = lax.axis_index("sta")
    has_prev = tm > 0
    has_next = tm < n_tm - 1
    is_last = tm == n_tm - 1

    copies = [
        pltpu.make_async_copy(traces, own, local_sem.at[0]),
        pltpu.make_async_copy(table_hbm, table, local_sem.at[1]),
        pltpu.make_async_copy(lag_hbm, lags, local_sem.at[2]),
    ]
    for copy in copies:
        copy.start()

    incoming[...] = jnp.zeros_like(incoming)
    offset_send[...] = jnp.full(offset_send.shape, offsets[2], jnp.int32)

    @pl.when(tm == 0)
    def _():
        rim_prev[...] = jnp.zeros_like(rim_prev)
        offset_recv[...] = jnp.full(offset_recv.shape, 2 * STEP, jnp.int32)

    @pl.when(is_last)
    def _():
        rim_next[...] = jnp.zeros_like(rim_next)

    barrier = pltpu.get_barrier_semaphore()
    for delta in range(1, n_sta):
        pl.semaphore_signal(
            barrier, inc=1, device_id={"sta": (me + delta) % n_sta}, device_id_type=MESH
        )

    @pl.when(has_prev)
    def _():
        pl.semaphore_signal(barrier, inc=1, device_id={"tm": tm - 1}, device_id_type=MESH)

    @pl.when(has_next)
    def _():
        pl.semaphore_signal(barrier, inc=1, device_id={"tm": tm + 1}, device_id_type=MESH)

    greeted = n_sta - 1 + has_prev.astype(jnp.int32) + has_next.astype(jnp.int32)
    pl.semaphore_wait(barrier, greeted)

    def rim_up(c):
        rows = pl.ds(c * chunk, chunk)
        return pltpu.make_async_remote_copy(
            src_ref=traces.at[rows, pl.ds(TB - STEP, STEP)],
            dst_ref=rim_prev.at[rows],
            send_sem=rim_send_sem.at[0, c],
            recv_sem=rim_recv_sem.at[0, c],
            device_id={"tm": tm + 1},
            device_id_type=MESH,
        )

    def rim_down(c):
        rows = pl.ds(c * chunk, chunk)
        return pltpu.make_async_remote_copy(
            src_ref=traces.at[rows, pl.ds(0, STEP)],
            dst_ref=rim_next.at[rows],
            send_sem=rim_send_sem.at[1, c],
            recv_sem=rim_recv_sem.at[1, c],
            device_id={"tm": tm - 1},
            device_id_type=MESH,
        )

    offset_up = pltpu.make_async_remote_copy(
        src_ref=offset_send,
        dst_ref=offset_recv,
        send_sem=offset_sem.at[0],
        recv_sem=offset_sem.at[1],
        device_id={"tm": tm + 1},
        device_id_type=MESH,
    )

    @pl.when(has_next)
    def _():
        offset_up.start()

    for c in range(CHUNKS):

        @pl.when(has_next)
        def _():
            rim_up(c).start()

        @pl.when(has_prev)
        def _():
            rim_down(c).start()

    def one_hot(values, count, depth):
        spread = jnp.transpose(
            jnp.broadcast_to(values.astype(jnp.float32), (BLK, count))
        )
        lane = lax.broadcasted_iota(jnp.int32, (count, BLK), 1).astype(jnp.float32)
        return [
            (spread == lane + float(b * BLK)).astype(jnp.float32).astype(jnp.bfloat16)
            for b in range(depth // BLK)
        ]

    for ref, values, count, depth in (
        (pick_first, pair_first, pairs, stations),
        (pick_second, pair_slot, pairs, slots),
        (pick_send, send_rows, slots, stations),
    ):
        for b, block in enumerate(one_hot(values[...], count, depth)):
            ref[:, b * BLK : (b + 1) * BLK] = block

    for copy in copies[:2]:
        copy.wait()

    batch = 2 * chunk

    def transform():
        spec[...] = jnp.dot(
            seg[...], table[...], preferred_element_type=jnp.float32
        ) * (1.0 / math.sqrt(WIN))

    def single_window(slot, jitter, blocks_at):
        @pl.loop(0, stations // batch)
        def _(step):
            start = step * batch

            @pl.loop(0, batch // ROWS)
            def _(g):
                row = pl.multiple_of(start + g * ROWS, ROWS)
                write_segment(
                    blocks_at(row), jitter, taper, seg, pl.multiple_of(g * ROWS, ROWS)
                )

            transform()

            @pl.loop(0, batch // ROWS)
            def _(g):
                re, im = whiten_rows(spec, pl.multiple_of(g * ROWS, ROWS))
                row = pl.multiple_of(start + g * ROWS, ROWS)
                white[slot, pl.ds(row, ROWS), :NF] = re
                white[slot, pl.ds(row, ROWS), NF:] = im

    def swap(which, slot, depth):
        result = []
        for delta in range(1, n_sta):
            rows = CAP if min(delta, n_sta - delta) <= 1 else FAR_ROWS
            partner = (me + delta) % n_sta
            result.append(
                pltpu.make_async_remote_copy(
                    src_ref=outgoing.at[
                        pl.ds(slot, depth), pl.ds(pl.multiple_of(partner * CAP, CAP), rows)
                    ],
                    dst_ref=incoming.at[
                        pl.ds(slot, depth), pl.ds(pl.multiple_of(me * CAP, CAP), rows)
                    ],
                    send_sem=swap_send_sem.at[which, delta],
                    recv_sem=swap_recv_sem.at[which, delta],
                    device_id={"sta": partner},
                    device_id_type=MESH,
                )
            )
        return result

    def start_swap(which, slot, depth):
        for w in range(slot, slot + depth):
            outgoing[w] = jnp.dot(
                pick_send[...], white[w], preferred_element_type=jnp.float32
            ).astype(jnp.bfloat16)
        for copy in swap(which, slot, depth):
            copy.start()
        mine = pl.ds(pl.multiple_of(me * CAP, CAP), CAP)
        for w in range(slot, slot + depth):
            incoming[w, mine] = outgoing[w, mine]

    def end_swap(which, slot, depth):
        for copy in swap(which, slot, depth):
            copy.wait()

    def gather_first(w):
        first_rows[w] = jnp.dot(
            pick_first[...], white[w], preferred_element_type=jnp.float32
        ).astype(jnp.bfloat16)

    part = min(pairs, 256)
    width = 256

    def add_cross(windows, fresh, final):
        @pl.loop(0, pairs // part)
        def _(p):
            rows = pl.ds(pl.multiple_of(p * part, part), part)
            for b in range(NF // width):
                rcol = slice(b * width, (b + 1) * width)
                icol = slice(NF + b * width, NF + (b + 1) * width)
                real = None if fresh else cross_sum[rows, rcol]
                imag = None if fresh else cross_sum[rows, icol]
                for w in windows:
                    fr = first_rows[w, rows, rcol].astype(jnp.float32)
                    fi = first_rows[w, rows, icol].astype(jnp.float32)
                    sr = jnp.dot(
                        pick_second[rows], incoming[w, :, rcol],
                        preferred_element_type=jnp.float32,
                    )
                    si = jnp.dot(
                        pick_second[rows], incoming[w, :, icol],
                        preferred_element_type=jnp.float32,
                    )
                    new_real = fr * sr + fi * si
                    new_imag = fi * sr - fr * si
                    real = new_real if real is None else real + new_real
                    imag = new_imag if imag is None else imag + new_imag
                if final:
                    cross[rows, rcol] = real.astype(jnp.bfloat16)
                    cross[rows, icol] = imag.astype(jnp.bfloat16)
                else:
                    cross_sum[rows, rcol] = real
                    cross_sum[rows, icol] = imag

    single_window(0, offsets[0], lambda row: load_blocks(own, row, 0, 24))
    start_swap(0, 0, 1)

    @pl.when(is_last)
    def _():
        single_window(
            3,
            offsets[2] - 2 * STEP,
            lambda row: load_blocks(own, row, 16, 8)
            + [jnp.zeros((ROWS, BLK), jnp.float32)] * 16,
        )
        start_swap(2, 3, 1)

    gather_first(0)
    end_swap(0, 0, 1)
    add_cross((0,), True, False)

    @pl.when(is_last)
    def _():
        gather_first(3)
        end_swap(2, 3, 1)
        add_cross((3,), False, False)

    @pl.when(has_prev)
    def _():
        offset_up.wait_recv()

    jitter_1 = offsets[1] - STEP
    jitter_2 = offset_recv[0, 0] - 2 * STEP
    keep = jnp.where(has_prev, 1.0, 0.0).astype(jnp.float32)

    @pl.loop(0, CHUNKS)
    def _(c):
        @pl.when(has_prev)
        def _():
            rim_up(c).wait_recv()

        @pl.when(has_next)
        def _():
            rim_down(c).wait_recv()

        start = c * chunk

        @pl.loop(0, chunk // ROWS)
        def _(g):
            row = pl.multiple_of(start + g * ROWS, ROWS)
            at = pl.multiple_of(g * ROWS, ROWS)
            write_segment(
                load_blocks(own, row, 8, 16) + load_blocks(rim_next, row, 0, 8),
                jitter_1, taper, seg, at,
            )
            write_segment(
                load_blocks(rim_prev, row, 0, 8) + load_blocks(own, row, 0, 16),
                jitter_2, taper, seg, pl.multiple_of(chunk + g * ROWS, ROWS),
            )

        transform()

        @pl.loop(0, chunk // ROWS)
        def _(g):
            row = pl.multiple_of(start + g * ROWS, ROWS)
            re, im = whiten_rows(spec, pl.multiple_of(g * ROWS, ROWS))
            white[1, pl.ds(row, ROWS), :NF] = re
            white[1, pl.ds(row, ROWS), NF:] = im
            re, im = whiten_rows(spec, pl.multiple_of(chunk + g * ROWS, ROWS))
            white[2, pl.ds(row, ROWS), :NF] = (re * keep).astype(jnp.bfloat16)
            white[2, pl.ds(row, ROWS), NF:] = (im * keep).astype(jnp.bfloat16)

    start_swap(1, 1, 2)
    gather_first(1)
    gather_first(2)
    copies[2].wait()
    end_swap(1, 1, 2)
    add_cross((1, 2), False, True)

    span = pairs // PIECES

    def share(c, piece):
        return lax.dot_general(
            lags[pl.ds(pl.multiple_of(c * lag_rows, lag_rows), lag_rows)],
            cross[pl.ds(pl.multiple_of(piece * span, span), span)],
            (((1,), (1,)), ((), ())),
            preferred_element_type=jnp.float32,
        )

    def up(index):
        return pltpu.make_async_remote_copy(
            src_ref=up_send.at[index],
            dst_ref=up_recv.at[index],
            send_sem=up_send_sem.at[index],
            recv_sem=up_recv_sem.at[index],
            device_id={"tm": tm + 1},
            device_id_type=MESH,
        )

    def down(index):
        return pltpu.make_async_remote_copy(
            src_ref=down_send.at[index],
            dst_ref=down_recv.at[index],
            send_sem=down_send_sem.at[index],
            recv_sem=down_recv_sem.at[index],
            device_id={"tm": tm - 1},
            device_id_type=MESH,
        )

    @pl.loop(0, (n_tm - 1) * PIECES)
    def _(t):
        up_item = t - tm
        up_chunk = n_tm - 1 - up_item // PIECES
        up_piece = up_item % PIECES

        @pl.when((up_item >= 0) & (up_item < (n_tm - 1 - tm) * PIECES))
        def _():
            index = up_chunk * PIECES + up_piece
            own_share = share(up_chunk, up_piece)

            @pl.when(has_prev)
            def _():
                up(index).wait_recv()
                up_send[index] = (own_share + up_recv[index].astype(jnp.float32)).astype(
                    jnp.bfloat16
                )

            @pl.when(tm == 0)
            def _():
                up_send[index] = own_share.astype(jnp.bfloat16)

            up(index).start()

        down_item = t - (n_tm - 1 - tm)
        down_chunk = down_item // PIECES
        down_piece = down_item % PIECES

        @pl.when((down_item >= 0) & (down_item < tm * PIECES))
        def _():
            index = down_chunk * PIECES + down_piece
            own_share = share(down_chunk, down_piece)

            @pl.when(has_next)
            def _():
                down(index).wait_recv()
                down_send[index] = (own_share + down_recv[index].astype(jnp.float32)).astype(
                    jnp.bfloat16
                )

            @pl.when(is_last)
            def _():
                down_send[index] = own_share.astype(jnp.bfloat16)

            down(index).start()

    scaling = 1.0 / math.sqrt(NF * 3 * n_tm)
    for piece in range(PIECES):
        index = tm * PIECES + piece
        columns = slice(piece * span, (piece + 1) * span)
        out[:, columns] = share(tm, piece) * scaling

    for piece in range(PIECES):
        index = tm * PIECES + piece
        columns = slice(piece * span, (piece + 1) * span)

        @pl.when(has_prev)
        def _():
            up(index).wait_recv()
            out[:, columns] += up_recv[index].astype(jnp.float32) * scaling

        @pl.when(has_next)
        def _():
            down(index).wait_recv()
            out[:, columns] += down_recv[index].astype(jnp.float32) * scaling

    @pl.when(has_next)
    def _():
        offset_up.wait_send()

    for c in range(CHUNKS):

        @pl.when(has_next)
        def _():
            rim_up(c).wait_send()

        @pl.when(has_prev)
        def _():
            rim_down(c).wait_send()

    @pl.loop(0, n_tm * PIECES)
    def _(index):
        @pl.when(index >= (tm + 1) * PIECES)
        def _():
            up(index).wait_send()

        @pl.when(index < tm * PIECES)
        def _():
            down(index).wait_send()


def on_device(n_tm, n_sta, traces, offsets, pair_first, pair_slot, send_rows):
    stations = traces.shape[0]
    pairs = pair_first.shape[0]
    slots = n_sta * CAP
    lag_rows = NL // n_tm
    chunk = stations // CHUNKS
    items = n_tm * PIECES
    bf16, f32 = jnp.bfloat16, jnp.float32
    vmem = pl.BlockSpec(memory_space=pltpu.VMEM)
    smem = pl.BlockSpec(memory_space=pltpu.SMEM)
    hbm = pl.BlockSpec(memory_space=pl.ANY)
    dma = pltpu.SemaphoreType.DMA
    strip = pltpu.VMEM((items, lag_rows, pairs // PIECES), bf16)
    return pl.pallas_call(
        functools.partial(kernel, n_tm, n_sta),
        out_shape=jax.ShapeDtypeStruct((lag_rows, pairs), f32),
        in_specs=[smem, vmem, vmem, vmem, vmem, hbm, hbm, hbm],
        out_specs=vmem,
        scratch_shapes=[
            pltpu.VMEM((stations, TB), bf16),
            pltpu.VMEM((stations, STEP), bf16),
            pltpu.VMEM((stations, STEP), bf16),
            pltpu.VMEM((WIN, 2 * NF), bf16),
            pltpu.VMEM((NL, 2 * NF), bf16),
            pltpu.VMEM((2 * chunk, WIN), bf16),
            pltpu.VMEM((2 * chunk, 2 * NF), f32),
            pltpu.VMEM((4, stations, 2 * NF), bf16),
            pltpu.VMEM((4, slots, 2 * NF), bf16),
            pltpu.VMEM((4, slots, 2 * NF), bf16),
            pltpu.VMEM((pairs, stations), bf16),
            pltpu.VMEM((pairs, slots), bf16),
            pltpu.VMEM((slots, stations), bf16),
            pltpu.VMEM((4, pairs, 2 * NF), bf16),
            pltpu.VMEM((pairs, 2 * NF), f32),
            pltpu.VMEM((pairs, 2 * NF), bf16),
            strip,
            strip,
            strip,
            strip,
            pltpu.VMEM((8, BLK), jnp.int32),
            pltpu.VMEM((8, BLK), jnp.int32),
            dma((3,)),
            dma((2, CHUNKS)),
            dma((2, CHUNKS)),
            dma((2,)),
            dma((3, n_sta)),
            dma((3, n_sta)),
            dma((items,)),
            dma((items,)),
            dma((items,)),
            dma((items,)),
        ],
        compiler_params=pltpu.CompilerParams(
            collective_id=0, has_side_effects=True, vmem_limit_bytes=56 * 1024 * 1024
        ),
    )(
        offsets,
        pair_first.reshape(1, pairs),
        pair_slot.reshape(1, pairs),
        send_rows,
        jnp.asarray(taper_table()),
        traces,
        jnp.asarray(dft_table()),
        jnp.asarray(lag_table()),
    )


def solution(mesh):
    in_specs = (P("sta", ("day", "tm")), P(("day", "tm")), P("sta"), P("sta"), P("sta", None))
    out_specs = P(("day", "tm"), "sta")
    return jax.shard_map(
        functools.partial(on_device, mesh.shape["tm"], mesh.shape["sta"]),
        mesh=mesh,
        in_specs=in_specs,
        out_specs=out_specs,
        check_vma=False,
    )
```

time: 258 us -> 91.5 us (0.35)
  Pallas kernels: 0 us -> 89.4 us
  other arithmetic: 88.7 us -> 0 us
  waiting for transfers between devices: 76.3 us -> 0 us
  local copies, waits for them, and re-layouts: 53.8 us -> 1.87 us
  matrix products: 19.3 us -> 0 us
  between operations: 13.6 us -> 0.01 us
  starting transfers between devices: 4.84 us -> 0 us
    pallas_call x0 -> x1, Pallas kernels: none -> 89.4 us  [on_device(): pl.pallas_call(functools.partial(kernel, n_tm, n_sta), out_shape=jax.Shap...]
    reduce_scatter x1 -> x0, waiting for transfers between devices: 43.4 us -> none  [on_device(): lax.psum_scatter(lax.dot_general(lag_rows, cross_sum, (((1,), (1,)), ((),...]
    gather x16 -> x0, local copies, waits for them, and re-layouts: 32.4 us -> none
    ppermute x1 -> x0, waiting for transfers between devices: 31.1 us -> none  [shifted(): return lax.ppermute(block, axis, route)]
    dot_general x2 -> x0, matrix products: 19.3 us -> none  [the longest x1 10.3 us: on_device(): lax.dot_general(lag_rows, cross_sum, (((1,), (1,)), ((), ())), precision=...]
    another operation x1 -> x0, other arithmetic: 18.3 us -> none
    convert_element_type x2 -> x0, other arithmetic: 17.1 us -> none  [the longest x1 12.6 us: whiten(): (spectrum * jnp.concatenate([inverse, inverse], axis=-1)).astype(jnp.bflo...]
    div x2 -> x0, other arithmetic: 16.7 us -> none  [the longest x1 16.7 us: whiten(): inverse = 1.0 / jnp.maximum(smooth, FLOOR)]
  transfers between devices with their start and end apart: 3 -> 0, of which waited for: 3 -> 0; matrix products, arithmetic and copies ran while one was open for 12% -> 0% of each run, Pallas kernels for 0% -> 0%
where the time goes in v1:
time: 91.5 us; the launch traced here: 91.3 us
  Pallas kernels  89.4 us (98%)
  local copies, waits for them, and re-layouts  1.87 us (2%)
    pallas_call x1, Pallas kernels, on_device(): pl.pallas_call(functools.partial(kernel, n_tm, n_sta), out_shape=jax.Shap...  89.4 us
    unnamed x1, local copies, waits for them, and re-layouts  1.87 us

profile of v1, /device:TPU:0, one launch (start us, length us, event | category | flops | bytes accessed | tf_op | source)
XLA Modules:
  0.0 91.3 jit_solution(1481367475401384090)
XLA Ops:
  0.0 89.4 %shard_map.82 = f32[256,512]{1,0:T(8,128)} custom-call(s32[3]{0:T(128)} %offsets.1, s32[1,512]{1,0:T(1,128)} %bitcast.2, s32[1,512]{1,0:T(1,128)} %bitcast.3, s32[1,128]{1,0:T(1,128)} %send_rows.1, f32[1,2048]{1,0:T(1,128)} %constant.6.clone.taper, bf16[512,3072]{1,0:T(8,128)(2,1)} %traces.1, bf16[2048,1024]{1,0:T(8,128)(2,1)} %constant.7.clone.table_hbm, ...), custom_call_target="tpu_custom_call" | custom-call | tf_op jit(solution)/shard_map/pallas_call | solution.py:528
  89.4 1.9 %copy.10 = f32[256,512]{1,0:T(8,128)} copy(f32[256,512]{1,0:T(8,128)} %shard_map.82) | data formatting | bytes 1048576

commit v2 on v1

--- a/solution.py
+++ b/solution.py
@@ -61,9 +61,10 @@
 
 def write_segment(blocks, jitter, taper, seg, row):
     values = shifted(blocks, jitter)
-    total = values[0]
-    for v in values[1:]:
-        total = total + v
+    sums = values
+    while len(sums) > 1:
+        sums = [a + b for a, b in zip(sums[::2], sums[1::2])]
+    total = sums[0]
     mean = jnp.sum(total, axis=1, keepdims=True) * (1.0 / WIN)
     for i, v in enumerate(values):
         columns = slice(i * BLK, (i + 1) * BLK)
@@ -225,7 +226,7 @@
         def _(step):
             start = step * batch
 
-            @pl.loop(0, batch // ROWS)
+            @pl.loop(0, batch // ROWS, unroll=4)
             def _(g):
                 row = pl.multiple_of(start + g * ROWS, ROWS)
                 write_segment(
@@ -234,7 +235,7 @@
 
             transform()
 
-            @pl.loop(0, batch // ROWS)
+            @pl.loop(0, batch // ROWS, unroll=4)
             def _(g):
                 re, im = whiten_rows(spec, pl.multiple_of(g * ROWS, ROWS))
                 row = pl.multiple_of(start + g * ROWS, ROWS)
@@ -359,7 +360,7 @@
 
         start = c * chunk
 
-        @pl.loop(0, chunk // ROWS)
+        @pl.loop(0, chunk // ROWS, unroll=2)
         def _(g):
             row = pl.multiple_of(start + g * ROWS, ROWS)
             at = pl.multiple_of(g * ROWS, ROWS)
@@ -374,7 +375,7 @@
 
         transform()
 
-        @pl.loop(0, chunk // ROWS)
+        @pl.loop(0, chunk // ROWS, unroll=2)
         def _(g):
             row = pl.multiple_of(start + g * ROWS, ROWS)
             re, im = whiten_rows(spec, pl.multiple_of(g * ROWS, ROWS))

time: 91.5 us -> 69.7 us (0.76)
  Pallas kernels: 89.4 us -> 67.6 us
    pallas_call x1, Pallas kernels: 89.4 us -> 67.6 us  [on_device(): pl.pallas_call(functools.partial(kernel, n_tm, n_sta), out_shape=jax.Shap...]
where the time goes in v2:
time: 69.7 us; the launch traced here: 69.5 us
  Pallas kernels  67.6 us (97%)
  local copies, waits for them, and re-layouts  1.87 us (3%)
    pallas_call x1, Pallas kernels, on_device(): pl.pallas_call(functools.partial(kernel, n_tm, n_sta), out_shape=jax.Shap...  67.6 us
    unnamed x1, local copies, waits for them, and re-layouts  1.87 us

profile of v2, /device:TPU:0, one launch (start us, length us, event | category | flops | bytes accessed | tf_op | source)
XLA Modules:
  0.0 69.5 jit_solution(17220058567097649640)
XLA Ops:
  0.0 67.6 %shard_map.82 = f32[256,512]{1,0:T(8,128)} custom-call(s32[3]{0:T(128)} %offsets.1, s32[1,512]{1,0:T(1,128)} %bitcast.2, s32[1,512]{1,0:T(1,128)} %bitcast.3, s32[1,128]{1,0:T(1,128)} %send_rows.1, f32[1,2048]{1,0:T(1,128)} %constant.6.clone.taper, bf16[512,3072]{1,0:T(8,128)(2,1)} %traces.1, bf16[2048,1024]{1,0:T(8,128)(2,1)} %constant.7.clone.table_hbm, ...), custom_call_target="tpu_custom_call" | custom-call | tf_op jit(solution)/shard_map/pallas_call | solution.py:529
  67.6 1.9 %copy.10 = f32[256,512]{1,0:T(8,128)} copy(f32[256,512]{1,0:T(8,128)} %shard_map.82) | data formatting | bytes 1048576

commit v3 on v2

--- a/solution.py
+++ b/solution.py
@@ -60,7 +60,7 @@
 
 
 def write_segment(blocks, jitter, taper, seg, row):
-    values = shifted(blocks, jitter)
+    values = [v.astype(jnp.float32) for v in shifted(blocks, jitter)]
     sums = values
     while len(sums) > 1:
         sums = [a + b for a, b in zip(sums[::2], sums[1::2])]
@@ -73,7 +73,7 @@
 
 def load_blocks(ref, row, first, count):
     return [
-        ref[pl.ds(row, ROWS), i * BLK : (i + 1) * BLK].astype(jnp.float32)
+        ref[pl.ds(row, ROWS), i * BLK : (i + 1) * BLK]
         for i in range(first, first + count)
     ]
 
@@ -214,11 +214,11 @@
     for copy in copies[:2]:
         copy.wait()
 
-    batch = 2 * chunk
-
-    def transform():
-        spec[...] = jnp.dot(
-            seg[...], table[...], preferred_element_type=jnp.float32
+    batch = stations
+
+    def transform(count):
+        spec[:count] = jnp.dot(
+            seg[:count], table[...], preferred_element_type=jnp.float32
         ) * (1.0 / math.sqrt(WIN))
 
     def single_window(slot, jitter, blocks_at):
@@ -233,7 +233,7 @@
                     blocks_at(row), jitter, taper, seg, pl.multiple_of(g * ROWS, ROWS)
                 )
 
-            transform()
+            transform(batch)
 
             @pl.loop(0, batch // ROWS, unroll=4)
             def _(g):
@@ -283,39 +283,42 @@
             pick_first[...], white[w], preferred_element_type=jnp.float32
         ).astype(jnp.bfloat16)
 
-    part = min(pairs, 256)
+    part = pairs // PIECES
     width = 256
 
-    def add_cross(windows, fresh, final):
-        @pl.loop(0, pairs // part)
+    def cross_part(p, windows, fresh, final):
+        rows = pl.ds(pl.multiple_of(p * part, part), part)
+        for b in range(NF // width):
+            rcol = slice(b * width, (b + 1) * width)
+            icol = slice(NF + b * width, NF + (b + 1) * width)
+            real = None if fresh else cross_sum[rows, rcol]
+            imag = None if fresh else cross_sum[rows, icol]
+            for w in windows:
+                fr = first_rows[w, rows, rcol].astype(jnp.float32)
+                fi = first_rows[w, rows, icol].astype(jnp.float32)
+                sr = jnp.dot(
+                    pick_second[rows], incoming[w, :, rcol],
+                    preferred_element_type=jnp.float32,
+                )
+                si = jnp.dot(
+                    pick_second[rows], incoming[w, :, icol],
+                    preferred_element_type=jnp.float32,
+                )
+                new_real = fr * sr + fi * si
+                new_imag = fi * sr - fr * si
+                real = new_real if real is None else real + new_real
+                imag = new_imag if imag is None else imag + new_imag
+            if final:
+                cross[rows, rcol] = real.astype(jnp.bfloat16)
+                cross[rows, icol] = imag.astype(jnp.bfloat16)
+            else:
+                cross_sum[rows, rcol] = real
+                cross_sum[rows, icol] = imag
+
+    def add_cross(windows, fresh):
+        @pl.loop(0, PIECES)
         def _(p):
-            rows = pl.ds(pl.multiple_of(p * part, part), part)
-            for b in range(NF // width):
-                rcol = slice(b * width, (b + 1) * width)
-                icol = slice(NF + b * width, NF + (b + 1) * width)
-                real = None if fresh else cross_sum[rows, rcol]
-                imag = None if fresh else cross_sum[rows, icol]
-                for w in windows:
-                    fr = first_rows[w, rows, rcol].astype(jnp.float32)
-                    fi = first_rows[w, rows, icol].astype(jnp.float32)
-                    sr = jnp.dot(
-                        pick_second[rows], incoming[w, :, rcol],
-                        preferred_element_type=jnp.float32,
-                    )
-                    si = jnp.dot(
-                        pick_second[rows], incoming[w, :, icol],
-                        preferred_element_type=jnp.float32,
-                    )
-                    new_real = fr * sr + fi * si
-                    new_imag = fi * sr - fr * si
-                    real = new_real if real is None else real + new_real
-                    imag = new_imag if imag is None else imag + new_imag
-                if final:
-                    cross[rows, rcol] = real.astype(jnp.bfloat16)
-                    cross[rows, icol] = imag.astype(jnp.bfloat16)
-                else:
-                    cross_sum[rows, rcol] = real
-                    cross_sum[rows, icol] = imag
+            cross_part(p, windows, fresh, False)
 
     single_window(0, offsets[0], lambda row: load_blocks(own, row, 0, 24))
     start_swap(0, 0, 1)
@@ -326,19 +329,19 @@
             3,
             offsets[2] - 2 * STEP,
             lambda row: load_blocks(own, row, 16, 8)
-            + [jnp.zeros((ROWS, BLK), jnp.float32)] * 16,
+            + [jnp.zeros((ROWS, BLK), jnp.bfloat16)] * 16,
         )
         start_swap(2, 3, 1)
 
     gather_first(0)
     end_swap(0, 0, 1)
-    add_cross((0,), True, False)
+    add_cross((0,), True)
 
     @pl.when(is_last)
     def _():
         gather_first(3)
         end_swap(2, 3, 1)
-        add_cross((3,), False, False)
+        add_cross((3,), False)
 
     @pl.when(has_prev)
     def _():
@@ -373,9 +376,9 @@
                 jitter_2, taper, seg, pl.multiple_of(chunk + g * ROWS, ROWS),
             )
 
-        transform()
-
-        @pl.loop(0, chunk // ROWS, unroll=2)
+        transform(2 * chunk)
+
+        @pl.loop(0, chunk // ROWS, unroll=4)
         def _(g):
             row = pl.multiple_of(start + g * ROWS, ROWS)
             re, im = whiten_rows(spec, pl.multiple_of(g * ROWS, ROWS))
@@ -390,7 +393,6 @@
     gather_first(2)
     copies[2].wait()
     end_swap(1, 1, 2)
-    add_cross((1, 2), False, True)
 
     span = pairs // PIECES
 
@@ -424,6 +426,10 @@
 
     @pl.loop(0, (n_tm - 1) * PIECES)
     def _(t):
+        @pl.when(t < PIECES)
+        def _():
+            cross_part(t, (1, 2), False, True)
+
         up_item = t - tm
         up_chunk = n_tm - 1 - up_item // PIECES
         up_piece = up_item % PIECES
@@ -537,8 +543,8 @@
             pltpu.VMEM((stations, STEP), bf16),
             pltpu.VMEM((WIN, 2 * NF), bf16),
             pltpu.VMEM((NL, 2 * NF), bf16),
-            pltpu.VMEM((2 * chunk, WIN), bf16),
-            pltpu.VMEM((2 * chunk, 2 * NF), f32),
+            pltpu.VMEM((stations, WIN), bf16),
+            pltpu.VMEM((stations, 2 * NF), f32),
             pltpu.VMEM((4, stations, 2 * NF), bf16),
             pltpu.VMEM((4, slots, 2 * NF), bf16),
             pltpu.VMEM((4, slots, 2 * NF), bf16),

time: 69.7 us -> 67.6 us (0.970)
  Pallas kernels: 67.6 us -> 65.5 us
    pallas_call x1, Pallas kernels: 67.6 us -> 65.5 us  [on_device(): pl.pallas_call(functools.partial(kernel, n_tm, n_sta), out_shape=jax.Shap...]
where the time goes in v3:
time: 67.6 us; the launch traced here: 67.4 us
  Pallas kernels  65.5 us (97%)
  local copies, waits for them, and re-layouts  1.87 us (3%)
    pallas_call x1, Pallas kernels, on_device(): pl.pallas_call(functools.partial(kernel, n_tm, n_sta), out_shape=jax.Shap...  65.5 us
    unnamed x1, local copies, waits for them, and re-layouts  1.87 us

profile of v3, /device:TPU:0, one launch (start us, length us, event | category | flops | bytes accessed | tf_op | source)
XLA Modules:
  0.0 67.4 jit_solution(1163668108718616231)
XLA Ops:
  0.0 65.5 %shard_map.82 = f32[256,512]{1,0:T(8,128)} custom-call(s32[3]{0:T(128)} %offsets.1, s32[1,512]{1,0:T(1,128)} %bitcast.2, s32[1,512]{1,0:T(1,128)} %bitcast.3, s32[1,128]{1,0:T(1,128)} %send_rows.1, f32[1,2048]{1,0:T(1,128)} %constant.6.clone.taper, bf16[512,3072]{1,0:T(8,128)(2,1)} %traces.1, bf16[2048,1024]{1,0:T(8,128)(2,1)} %constant.7.clone.table_hbm, ...), custom_call_target="tpu_custom_call" | custom-call | tf_op jit(solution)/shard_map/pallas_call | solution.py:535
  65.5 1.9 %copy.10 = f32[256,512]{1,0:T(8,128)} copy(f32[256,512]{1,0:T(8,128)} %shard_map.82) | data formatting | bytes 1048576

commit v4 on v3

--- a/solution.py
+++ b/solution.py
@@ -94,8 +94,8 @@
     n_tm, n_sta,
     offsets, pair_first, pair_slot, send_rows, taper, traces, table_hbm, lag_hbm,
     out,
-    own, rim_prev, rim_next, table, lags, seg, spec, white, outgoing, incoming,
-    pick_first, pick_second, pick_send, first_rows, cross_sum, cross,
+    raw, own, rim_prev, rim_next, table, lags, seg, spec, white, outgoing, incoming,
+    pick_first, pick_second, pick_send, order, first_at, send_at, second_rows, cross_sum, cross,
     up_send, up_recv, down_send, down_recv, offset_send, offset_recv,
     local_sem, rim_send_sem, rim_recv_sem, offset_sem, swap_send_sem, swap_recv_sem,
     up_send_sem, up_recv_sem, down_send_sem, down_recv_sem,
@@ -105,6 +105,8 @@
     lag_rows = out.shape[0]
     slots = n_sta * CAP
     chunk = stations // CHUNKS
+    half = chunk // 2
+    early = slots <= chunk
     tm = lax.axis_index("tm")
     me = lax.axis_index("sta")
     has_prev = tm > 0
@@ -112,7 +114,7 @@
     is_last = tm == n_tm - 1
 
     copies = [
-        pltpu.make_async_copy(traces, own, local_sem.at[0]),
+        pltpu.make_async_copy(traces, raw, local_sem.at[0]),
         pltpu.make_async_copy(table_hbm, table, local_sem.at[1]),
         pltpu.make_async_copy(lag_hbm, lags, local_sem.at[2]),
     ]
@@ -145,13 +147,15 @@
     def _():
         pl.semaphore_signal(barrier, inc=1, device_id={"tm": tm + 1}, device_id_type=MESH)
 
-    greeted = n_sta - 1 + has_prev.astype(jnp.int32) + has_next.astype(jnp.int32)
-    pl.semaphore_wait(barrier, greeted)
+    def rim_rows(c):
+        if isinstance(c, int) and c >= CHUNKS - 1:
+            return pl.ds((CHUNKS - 1) * chunk + (c - CHUNKS + 1) * half, half)
+        return pl.ds(c * chunk, chunk)
 
     def rim_up(c):
-        rows = pl.ds(c * chunk, chunk)
+        rows = rim_rows(c)
         return pltpu.make_async_remote_copy(
-            src_ref=traces.at[rows, pl.ds(TB - STEP, STEP)],
+            src_ref=own.at[rows, pl.ds(TB - STEP, STEP)],
             dst_ref=rim_prev.at[rows],
             send_sem=rim_send_sem.at[0, c],
             recv_sem=rim_recv_sem.at[0, c],
@@ -160,9 +164,9 @@
         )
 
     def rim_down(c):
-        rows = pl.ds(c * chunk, chunk)
+        rows = rim_rows(c)
         return pltpu.make_async_remote_copy(
-            src_ref=traces.at[rows, pl.ds(0, STEP)],
+            src_ref=own.at[rows, pl.ds(0, STEP)],
             dst_ref=rim_next.at[rows],
             send_sem=rim_send_sem.at[1, c],
             recv_sem=rim_recv_sem.at[1, c],
@@ -179,11 +183,50 @@
         device_id_type=MESH,
     )
 
-    @pl.when(has_next)
-    def _():
-        offset_up.start()
-
-    for c in range(CHUNKS):
+    def one_hot(ref, values, depth):
+        count = values.shape[1]
+        spread = jnp.transpose(jnp.broadcast_to(values.astype(jnp.float32), (BLK, count)))
+        lane = lax.broadcasted_iota(jnp.int32, (count, BLK), 1).astype(jnp.float32)
+        for b in range(depth // BLK):
+            ref[:, b * BLK : (b + 1) * BLK] = (
+                (spread == lane + float(b * BLK)).astype(jnp.float32).astype(jnp.bfloat16)
+            )
+
+    one_hot(pick_send, send_rows[...], stations)
+    hits = jnp.dot(
+        jnp.ones((8, slots), jnp.bfloat16), pick_send[...], preferred_element_type=jnp.float32
+    )
+    chosen = hits > 0.5
+    mark = chosen.astype(jnp.float32)
+    from_row = lax.broadcasted_iota(jnp.int32, (stations, stations), 0)
+    to_lane = lax.broadcasted_iota(jnp.int32, (stations, stations), 1)
+    up_to = (from_row <= to_lane).astype(jnp.float32).astype(jnp.bfloat16)
+    running = jnp.dot(mark.astype(jnp.bfloat16), up_to, preferred_element_type=jnp.float32)
+    lane = lax.broadcasted_iota(jnp.int32, (8, stations), 1).astype(jnp.float32)
+    total = jnp.sum(mark, axis=1, keepdims=True)
+    place = jnp.where(chosen, running - 1.0, total + lane - running)
+    order[...] = (
+        (place[:1] == from_row.astype(jnp.float32)).astype(jnp.float32).astype(jnp.bfloat16)
+    )
+
+    copies[0].wait()
+
+    def arrange(rows, columns):
+        own[rows, columns] = jnp.dot(
+            order[rows], raw[:, columns], preferred_element_type=jnp.float32
+        ).astype(jnp.bfloat16)
+
+    for c in range(CHUNKS + 1):
+        arrange(rim_rows(c), slice(0, STEP))
+        arrange(rim_rows(c), slice(TB - STEP, TB))
+
+        if c == 0:
+            greeted = n_sta - 1 + has_prev.astype(jnp.int32) + has_next.astype(jnp.int32)
+            pl.semaphore_wait(barrier, greeted)
+
+            @pl.when(has_next)
+            def _():
+                offset_up.start()
 
         @pl.when(has_next)
         def _():
@@ -193,26 +236,19 @@
         def _():
             rim_down(c).start()
 
-    def one_hot(values, count, depth):
-        spread = jnp.transpose(
-            jnp.broadcast_to(values.astype(jnp.float32), (BLK, count))
-        )
-        lane = lax.broadcasted_iota(jnp.int32, (count, BLK), 1).astype(jnp.float32)
-        return [
-            (spread == lane + float(b * BLK)).astype(jnp.float32).astype(jnp.bfloat16)
-            for b in range(depth // BLK)
-        ]
-
-    for ref, values, count, depth in (
-        (pick_first, pair_first, pairs, stations),
-        (pick_second, pair_slot, pairs, slots),
-        (pick_send, send_rows, slots, stations),
-    ):
-        for b, block in enumerate(one_hot(values[...], count, depth)):
-            ref[:, b * BLK : (b + 1) * BLK] = block
-
-    for copy in copies[:2]:
-        copy.wait()
+    arrange(slice(0, stations), slice(STEP, TB - STEP))
+
+    def in_order(ref):
+        return lax.dot_general(
+            ref[...], order[...], (((1,), (1,)), ((), ())),
+            preferred_element_type=jnp.float32,
+        ).astype(jnp.bfloat16)
+
+    one_hot(pick_first, pair_first[...], stations)
+    one_hot(pick_second, pair_slot[...], slots)
+    first_at[...] = in_order(pick_first)
+    send_at[...] = in_order(pick_send)
+    copies[1].wait()
 
     batch = stations
 
@@ -263,10 +299,12 @@
             )
         return result
 
+    lead = min(slots, stations)
+
     def start_swap(which, slot, depth):
         for w in range(slot, slot + depth):
             outgoing[w] = jnp.dot(
-                pick_send[...], white[w], preferred_element_type=jnp.float32
+                send_at[:, :lead], white[w, :lead], preferred_element_type=jnp.float32
             ).astype(jnp.bfloat16)
         for copy in swap(which, slot, depth):
             copy.start()
@@ -277,16 +315,15 @@
     def end_swap(which, slot, depth):
         for copy in swap(which, slot, depth):
             copy.wait()
-
-    def gather_first(w):
-        first_rows[w] = jnp.dot(
-            pick_first[...], white[w], preferred_element_type=jnp.float32
-        ).astype(jnp.bfloat16)
+        for w in range(slot, slot + depth):
+            second_rows[w] = jnp.dot(
+                pick_second[...], incoming[w], preferred_element_type=jnp.float32
+            ).astype(jnp.bfloat16)
 
     part = pairs // PIECES
     width = 256
 
-    def cross_part(p, windows, fresh, final):
+    def cross_part(p, windows, low, high, fresh=False, final=False):
         rows = pl.ds(pl.multiple_of(p * part, part), part)
         for b in range(NF // width):
             rcol = slice(b * width, (b + 1) * width)
@@ -294,16 +331,15 @@
             real = None if fresh else cross_sum[rows, rcol]
             imag = None if fresh else cross_sum[rows, icol]
             for w in windows:
-                fr = first_rows[w, rows, rcol].astype(jnp.float32)
-                fi = first_rows[w, rows, icol].astype(jnp.float32)
-                sr = jnp.dot(
-                    pick_second[rows], incoming[w, :, rcol],
-                    preferred_element_type=jnp.float32,
-                )
-                si = jnp.dot(
-                    pick_second[rows], incoming[w, :, icol],
-                    preferred_element_type=jnp.float32,
-                )
+                fr, fi = [
+                    jnp.dot(
+                        first_at[rows, low:high], white[w, low:high, columns],
+                        preferred_element_type=jnp.float32,
+                    )
+                    for columns in (rcol, icol)
+                ]
+                sr = second_rows[w, rows, rcol].astype(jnp.float32)
+                si = second_rows[w, rows, icol].astype(jnp.float32)
                 new_real = fr * sr + fi * si
                 new_imag = fi * sr - fr * si
                 real = new_real if real is None else real + new_real
@@ -315,10 +351,10 @@
                 cross_sum[rows, rcol] = real
                 cross_sum[rows, icol] = imag
 
-    def add_cross(windows, fresh):
+    def add_cross(windows, low, high, fresh=False):
         @pl.loop(0, PIECES)
         def _(p):
-            cross_part(p, windows, fresh, False)
+            cross_part(p, windows, low, high, fresh=fresh)
 
     single_window(0, offsets[0], lambda row: load_blocks(own, row, 0, 24))
     start_swap(0, 0, 1)
@@ -333,16 +369,6 @@
         )
         start_swap(2, 3, 1)
 
-    gather_first(0)
-    end_swap(0, 0, 1)
-    add_cross((0,), True)
-
-    @pl.when(is_last)
-    def _():
-        gather_first(3)
-        end_swap(2, 3, 1)
-        add_cross((3,), False)
-
     @pl.when(has_prev)
     def _():
         offset_up.wait_recv()
@@ -351,8 +377,7 @@
     jitter_2 = offset_recv[0, 0] - 2 * STEP
     keep = jnp.where(has_prev, 1.0, 0.0).astype(jnp.float32)
 
-    @pl.loop(0, CHUNKS)
-    def _(c):
+    def two_windows(c, start, size):
         @pl.when(has_prev)
         def _():
             rim_up(c).wait_recv()
@@ -361,9 +386,7 @@
         def _():
             rim_down(c).wait_recv()
 
-        start = c * chunk
-
-        @pl.loop(0, chunk // ROWS, unroll=2)
+        @pl.loop(0, size // ROWS, unroll=2)
         def _(g):
             row = pl.multiple_of(start + g * ROWS, ROWS)
             at = pl.multiple_of(g * ROWS, ROWS)
@@ -373,26 +396,50 @@
             )
             write_segment(
                 load_blocks(rim_prev, row, 0, 8) + load_blocks(own, row, 0, 16),
-                jitter_2, taper, seg, pl.multiple_of(chunk + g * ROWS, ROWS),
+                jitter_2, taper, seg, pl.multiple_of(size + g * ROWS, ROWS),
             )
 
-        transform(2 * chunk)
-
-        @pl.loop(0, chunk // ROWS, unroll=4)
+        transform(2 * size)
+
+        @pl.loop(0, size // ROWS, unroll=2)
         def _(g):
             row = pl.multiple_of(start + g * ROWS, ROWS)
             re, im = whiten_rows(spec, pl.multiple_of(g * ROWS, ROWS))
             white[1, pl.ds(row, ROWS), :NF] = re
             white[1, pl.ds(row, ROWS), NF:] = im
-            re, im = whiten_rows(spec, pl.multiple_of(chunk + g * ROWS, ROWS))
+            re, im = whiten_rows(spec, pl.multiple_of(size + g * ROWS, ROWS))
             white[2, pl.ds(row, ROWS), :NF] = (re * keep).astype(jnp.bfloat16)
             white[2, pl.ds(row, ROWS), NF:] = (im * keep).astype(jnp.bfloat16)
 
-    start_swap(1, 1, 2)
-    gather_first(1)
-    gather_first(2)
+    def finish_early_windows():
+        end_swap(0, 0, 1)
+        add_cross((0,), 0, stations, fresh=True)
+
+        @pl.when(is_last)
+        def _():
+            end_swap(2, 3, 1)
+            add_cross((3,), 0, stations)
+
+    two_windows(0, 0, chunk)
+    if early:
+        start_swap(1, 1, 2)
+    finish_early_windows()
+
+    @pl.loop(1, CHUNKS - 1)
+    def _(c):
+        two_windows(c, c * chunk, chunk)
+
+    last_half = stations - half
+    two_windows(CHUNKS - 1, last_half - half, half)
+    if early:
+        end_swap(1, 1, 2)
+        add_cross((1, 2), 0, last_half)
+    two_windows(CHUNKS, last_half, half)
+    if not early:
+        start_swap(1, 1, 2)
+        end_swap(1, 1, 2)
     copies[2].wait()
-    end_swap(1, 1, 2)
+    pending = last_half if early else 0
 
     span = pairs // PIECES
 
@@ -428,7 +475,7 @@
     def _(t):
         @pl.when(t < PIECES)
         def _():
-            cross_part(t, (1, 2), False, True)
+            cross_part(t, (1, 2), pending, stations, final=True)
 
         up_item = t - tm
         up_chunk = n_tm - 1 - up_item // PIECES
@@ -498,7 +545,7 @@
     def _():
         offset_up.wait_send()
 
-    for c in range(CHUNKS):
+    for c in range(CHUNKS + 1):
 
         @pl.when(has_next)
         def _():
@@ -539,6 +586,7 @@
         out_specs=vmem,
         scratch_shapes=[
             pltpu.VMEM((stations, TB), bf16),
+            pltpu.VMEM((stations, TB), bf16),
             pltpu.VMEM((stations, STEP), bf16),
             pltpu.VMEM((stations, STEP), bf16),
             pltpu.VMEM((WIN, 2 * NF), bf16),
@@ -551,6 +599,9 @@
             pltpu.VMEM((pairs, stations), bf16),
             pltpu.VMEM((pairs, slots), bf16),
             pltpu.VMEM((slots, stations), bf16),
+            pltpu.VMEM((stations, stations), bf16),
+            pltpu.VMEM((pairs, stations), bf16),
+            pltpu.VMEM((slots, stations), bf16),
             pltpu.VMEM((4, pairs, 2 * NF), bf16),
             pltpu.VMEM((pairs, 2 * NF), f32),
             pltpu.VMEM((pairs, 2 * NF), bf16),
@@ -561,8 +612,8 @@
             pltpu.VMEM((8, BLK), jnp.int32),
             pltpu.VMEM((8, BLK), jnp.int32),
             dma((3,)),
-            dma((2, CHUNKS)),
-            dma((2, CHUNKS)),
+            dma((2, CHUNKS + 1)),
+            dma((2, CHUNKS + 1)),
             dma((2,)),
             dma((3, n_sta)),
             dma((3, n_sta)),

time: 67.6 us -> 64.2 us (0.950)
  Pallas kernels: 65.5 us -> 62.1 us
    pallas_call x1, Pallas kernels: 65.5 us -> 62.1 us  [on_device(): pl.pallas_call(functools.partial(kernel, n_tm, n_sta), out_shape=jax.Shap...]
where the time goes in v4:
time: 64.2 us; the launch traced here: 64 us
  Pallas kernels  62.1 us (97%)
  local copies, waits for them, and re-layouts  1.87 us (3%)
    pallas_call x1, Pallas kernels, on_device(): pl.pallas_call(functools.partial(kernel, n_tm, n_sta), out_shape=jax.Shap...  62.1 us
    unnamed x1, local copies, waits for them, and re-layouts  1.87 us

profile of v4, /device:TPU:0, one launch (start us, length us, event | category | flops | bytes accessed | tf_op | source)
XLA Modules:
  0.0 64.0 jit_solution(11999216157547104880)
XLA Ops:
  0.0 62.1 %shard_map.82 = f32[256,512]{1,0:T(8,128)} custom-call(s32[3]{0:T(128)} %offsets.1, s32[1,512]{1,0:T(1,128)} %bitcast.2, s32[1,512]{1,0:T(1,128)} %bitcast.3, s32[1,128]{1,0:T(1,128)} %send_rows.1, f32[1,2048]{1,0:T(1,128)} %constant.6.clone.taper, bf16[512,3072]{1,0:T(8,128)(2,1)} %traces.1, bf16[2048,1024]{1,0:T(8,128)(2,1)} %constant.7.clone.table_hbm, ...), custom_call_target="tpu_custom_call" | custom-call | tf_op jit(solution)/shard_map/pallas_call | solution.py:582
  62.1 1.9 %copy.10 = f32[256,512]{1,0:T(8,128)} copy(f32[256,512]{1,0:T(8,128)} %shard_map.82) | data formatting | bytes 1048576

commit v5 on v4

--- a/solution.py
+++ b/solution.py
@@ -18,7 +18,7 @@
 FAR_ROWS = 16
 FLOOR = 0.1
 CHUNKS = 4
-PIECES = 2
+PIECES = 4
 BLK = 128
 ROWS = 16
 MESH = pl.DeviceIdType.MESH
@@ -44,9 +44,10 @@
 
 
 def shifted(blocks, jitter):
+    wanted = len(blocks) - 8
     quotient = jitter // BLK
     rest = jitter % BLK
-    for bit, count in ((8, 24), (4, 20), (2, 18), (1, 17)):
+    for bit, count in ((8, wanted + 8), (4, wanted + 4), (2, wanted + 2), (1, wanted + 1)):
         on = (quotient // bit) % 2 == 1
         blocks = [
             jnp.where(on, blocks[i + bit], blocks[i]) if i + bit < len(blocks) else blocks[i]
@@ -56,19 +57,26 @@
     rolled = [pltpu.roll(b, turn, 1) for b in blocks]
     lane = lax.broadcasted_iota(jnp.int32, blocks[0].shape, 1)
     keep = lane < BLK - rest
-    return [jnp.where(keep, rolled[i], rolled[i + 1]) for i in range(WIN // BLK)]
-
-
-def write_segment(blocks, jitter, taper, seg, row):
+    return [jnp.where(keep, rolled[i], rolled[i + 1]) for i in range(wanted)]
+
+
+def write_segment(blocks, jitter, taper, seg, row, means=None):
     values = [v.astype(jnp.float32) for v in shifted(blocks, jitter)]
     sums = values
     while len(sums) > 1:
         sums = [a + b for a, b in zip(sums[::2], sums[1::2])]
     total = sums[0]
     mean = jnp.sum(total, axis=1, keepdims=True) * (1.0 / WIN)
+    if means is not None:
+        means[pl.ds(row, ROWS)] = jnp.broadcast_to(mean, (ROWS, BLK))
     for i, v in enumerate(values):
         columns = slice(i * BLK, (i + 1) * BLK)
         seg[pl.ds(row, ROWS), columns] = ((v - mean) * taper[:, columns]).astype(jnp.bfloat16)
+
+
+def taper_rest():
+    rest = taper_table()[0, STEP:].astype(np.float64) @ dft_table()[STEP:].astype(np.float64)
+    return rest.astype(np.float32)[None, :]
 
 
 def load_blocks(ref, row, first, count):
@@ -92,9 +100,9 @@
 
 def kernel(
     n_tm, n_sta,
-    offsets, pair_first, pair_slot, send_rows, taper, traces, table_hbm, lag_hbm,
+    offsets, pair_first, pair_slot, send_rows, taper, rest, traces, table_hbm, lag_hbm,
     out,
-    raw, own, rim_prev, rim_next, table, lags, seg, spec, white, outgoing, incoming,
+    raw, own, rim_prev, rim_next, table, lags, seg, spec, means, white, outgoing, incoming,
     pick_first, pick_second, pick_send, order, first_at, send_at, second_rows, cross_sum, cross,
     up_send, up_recv, down_send, down_recv, offset_send, offset_recv,
     local_sem, rim_send_sem, rim_recv_sem, offset_sem, swap_send_sem, swap_recv_sem,
@@ -113,13 +121,19 @@
     has_next = tm < n_tm - 1
     is_last = tm == n_tm - 1
 
-    copies = [
-        pltpu.make_async_copy(traces, raw, local_sem.at[0]),
-        pltpu.make_async_copy(table_hbm, table, local_sem.at[1]),
-        pltpu.make_async_copy(lag_hbm, lags, local_sem.at[2]),
-    ]
-    for copy in copies:
-        copy.start()
+    def load_columns(first, last, index):
+        columns = pl.ds(first, last - first)
+        return pltpu.make_async_copy(
+            traces.at[:, columns], raw.at[:, columns], local_sem.at[index]
+        )
+
+    load_head = load_columns(0, STEP, 0)
+    load_tail = load_columns(TB - STEP, TB, 1)
+    load_middle = load_columns(STEP, TB - STEP, 2)
+    load_table = pltpu.make_async_copy(table_hbm, table, local_sem.at[3])
+    load_lags = pltpu.make_async_copy(lag_hbm, lags, local_sem.at[4])
+    load_head.start()
+    load_tail.start()
 
     incoming[...] = jnp.zeros_like(incoming)
     offset_send[...] = jnp.full(offset_send.shape, offsets[2], jnp.int32)
@@ -209,7 +223,11 @@
         (place[:1] == from_row.astype(jnp.float32)).astype(jnp.float32).astype(jnp.bfloat16)
     )
 
-    copies[0].wait()
+    load_head.wait()
+    load_tail.wait()
+    load_middle.start()
+    load_table.start()
+    load_lags.start()
 
     def arrange(rows, columns):
         own[rows, columns] = jnp.dot(
@@ -236,6 +254,7 @@
         def _():
             rim_down(c).start()
 
+    load_middle.wait()
     arrange(slice(0, stations), slice(STEP, TB - STEP))
 
     def in_order(ref):
@@ -248,35 +267,40 @@
     one_hot(pick_second, pair_slot[...], slots)
     first_at[...] = in_order(pick_first)
     send_at[...] = in_order(pick_send)
-    copies[1].wait()
-
-    batch = stations
+    load_table.wait()
+
+    scale = 1.0 / math.sqrt(WIN)
 
     def transform(count):
-        spec[:count] = jnp.dot(
-            seg[:count], table[...], preferred_element_type=jnp.float32
-        ) * (1.0 / math.sqrt(WIN))
-
-    def single_window(slot, jitter, blocks_at):
-        @pl.loop(0, stations // batch)
-        def _(step):
-            start = step * batch
-
-            @pl.loop(0, batch // ROWS, unroll=4)
-            def _(g):
-                row = pl.multiple_of(start + g * ROWS, ROWS)
-                write_segment(
-                    blocks_at(row), jitter, taper, seg, pl.multiple_of(g * ROWS, ROWS)
-                )
-
-            transform(batch)
-
-            @pl.loop(0, batch // ROWS, unroll=4)
-            def _(g):
-                re, im = whiten_rows(spec, pl.multiple_of(g * ROWS, ROWS))
-                row = pl.multiple_of(start + g * ROWS, ROWS)
-                white[slot, pl.ds(row, ROWS), :NF] = re
-                white[slot, pl.ds(row, ROWS), NF:] = im
+        spec[:count] = (
+            jnp.dot(seg[:count], table[...], preferred_element_type=jnp.float32) * scale
+        )
+
+    def transform_half():
+        first = jnp.dot(
+            seg[:, :STEP], table[:STEP], preferred_element_type=jnp.float32
+        )
+        spec[...] = (first - means[:, :1] * rest[...]) * scale
+
+    def single_window(slot, jitter, blocks_at, half_window=False):
+        @pl.loop(0, stations // ROWS, unroll=4)
+        def _(g):
+            row = pl.multiple_of(g * ROWS, ROWS)
+            write_segment(
+                blocks_at(row), jitter, taper, seg, row, means if half_window else None
+            )
+
+        if half_window:
+            transform_half()
+        else:
+            transform(stations)
+
+        @pl.loop(0, stations // ROWS, unroll=4)
+        def _(g):
+            row = pl.multiple_of(g * ROWS, ROWS)
+            re, im = whiten_rows(spec, row)
+            white[slot, pl.ds(row, ROWS), :NF] = re
+            white[slot, pl.ds(row, ROWS), NF:] = im
 
     def swap(which, slot, depth):
         result = []
@@ -365,7 +389,8 @@
             3,
             offsets[2] - 2 * STEP,
             lambda row: load_blocks(own, row, 16, 8)
-            + [jnp.zeros((ROWS, BLK), jnp.bfloat16)] * 16,
+            + [jnp.zeros((ROWS, BLK), jnp.bfloat16)] * 8,
+            half_window=True,
         )
         start_swap(2, 3, 1)
 
@@ -429,17 +454,17 @@
     def _(c):
         two_windows(c, c * chunk, chunk)
 
-    last_half = stations - half
-    two_windows(CHUNKS - 1, last_half - half, half)
+    last = stations - chunk
     if early:
         end_swap(1, 1, 2)
-        add_cross((1, 2), 0, last_half)
-    two_windows(CHUNKS, last_half, half)
+        add_cross((1, 2), 0, last)
+    two_windows(CHUNKS - 1, last, half)
+    two_windows(CHUNKS, last + half, half)
     if not early:
         start_swap(1, 1, 2)
         end_swap(1, 1, 2)
-    copies[2].wait()
-    pending = last_half if early else 0
+    load_lags.wait()
+    pending = last if early else 0
 
     span = pairs // PIECES
 
@@ -582,7 +607,7 @@
     return pl.pallas_call(
         functools.partial(kernel, n_tm, n_sta),
         out_shape=jax.ShapeDtypeStruct((lag_rows, pairs), f32),
-        in_specs=[smem, vmem, vmem, vmem, vmem, hbm, hbm, hbm],
+        in_specs=[smem, vmem, vmem, vmem, vmem, vmem, hbm, hbm, hbm],
         out_specs=vmem,
         scratch_shapes=[
             pltpu.VMEM((stations, TB), bf16),
@@ -593,6 +618,7 @@
             pltpu.VMEM((NL, 2 * NF), bf16),
             pltpu.VMEM((stations, WIN), bf16),
             pltpu.VMEM((stations, 2 * NF), f32),
+            pltpu.VMEM((stations, BLK), f32),
             pltpu.VMEM((4, stations, 2 * NF), bf16),
             pltpu.VMEM((4, slots, 2 * NF), bf16),
             pltpu.VMEM((4, slots, 2 * NF), bf16),
@@ -611,7 +637,7 @@
             strip,
             pltpu.VMEM((8, BLK), jnp.int32),
             pltpu.VMEM((8, BLK), jnp.int32),
-            dma((3,)),
+            dma((5,)),
             dma((2, CHUNKS + 1)),
             dma((2, CHUNKS + 1)),
             dma((2,)),
@@ -631,6 +657,7 @@
         pair_slot.reshape(1, pairs),
         send_rows,
         jnp.asarray(taper_table()),
+        jnp.asarray(taper_rest()),
         traces,
         jnp.asarray(dft_table()),
         jnp.asarray(lag_table()),

time: 64.2 us -> 65.7 us (1.023)
  Pallas kernels: 62.1 us -> 63.6 us
    pallas_call x1, Pallas kernels: 62.1 us -> 63.6 us  [on_device(): pl.pallas_call(functools.partial(kernel, n_tm, n_sta), out_shape=jax.Shap...]
where the time goes in v5:
time: 65.7 us; the launch traced here: 65.4 us
  Pallas kernels  63.6 us (97%)
  local copies, waits for them, and re-layouts  1.87 us (3%)
    pallas_call x1, Pallas kernels, on_device(): pl.pallas_call(functools.partial(kernel, n_tm, n_sta), out_shape=jax.Shap...  63.6 us
    unnamed x1, local copies, waits for them, and re-layouts  1.87 us

profile of v5, /device:TPU:0, one launch (start us, length us, event | category | flops | bytes accessed | tf_op | source)
XLA Modules:
  0.0 65.4 jit_solution(2439679810223405101)
XLA Ops:
  0.0 63.6 %shard_map.91 = f32[256,512]{1,0:T(8,128)} custom-call(s32[3]{0:T(128)} %offsets.1, s32[1,512]{1,0:T(1,128)} %bitcast.2, s32[1,512]{1,0:T(1,128)} %bitcast.3, s32[1,128]{1,0:T(1,128)} %send_rows.1, f32[1,2048]{1,0:T(1,128)} %constant.8.clone.taper, f32[1,1024]{1,0:T(1,128)} %constant.9.clone.rest, bf16[512,3072]{1,0:T(8,128)(2,1)} %traces.1, ...), custom_call_target="tpu_custom_call" | custom-call | tf_op jit(solution)/shard_map/pallas_call | solution.py:607
  63.6 1.9 %copy.11 = f32[256,512]{1,0:T(8,128)} copy(f32[256,512]{1,0:T(8,128)} %shard_map.91) | data formatting | bytes 1048576

commit v6 on v5

--- a/solution.py
+++ b/solution.py
@@ -18,7 +18,7 @@
 FAR_ROWS = 16
 FLOOR = 0.1
 CHUNKS = 4
-PIECES = 4
+PIECES = 2
 BLK = 128
 ROWS = 16
 MESH = pl.DeviceIdType.MESH
@@ -166,10 +166,13 @@
             return pl.ds((CHUNKS - 1) * chunk + (c - CHUNKS + 1) * half, half)
         return pl.ds(c * chunk, chunk)
 
+    def source(c):
+        return traces if isinstance(c, int) and c == 0 else own
+
     def rim_up(c):
         rows = rim_rows(c)
         return pltpu.make_async_remote_copy(
-            src_ref=own.at[rows, pl.ds(TB - STEP, STEP)],
+            src_ref=source(c).at[rows, pl.ds(TB - STEP, STEP)],
             dst_ref=rim_prev.at[rows],
             send_sem=rim_send_sem.at[0, c],
             recv_sem=rim_recv_sem.at[0, c],
@@ -180,7 +183,7 @@
     def rim_down(c):
         rows = rim_rows(c)
         return pltpu.make_async_remote_copy(
-            src_ref=own.at[rows, pl.ds(0, STEP)],
+            src_ref=source(c).at[rows, pl.ds(0, STEP)],
             dst_ref=rim_next.at[rows],
             send_sem=rim_send_sem.at[1, c],
             recv_sem=rim_recv_sem.at[1, c],
@@ -197,6 +200,18 @@
         device_id_type=MESH,
     )
 
+    greeted = n_sta - 1 + has_prev.astype(jnp.int32) + has_next.astype(jnp.int32)
+    pl.semaphore_wait(barrier, greeted)
+
+    @pl.when(has_next)
+    def _():
+        rim_up(0).start()
+        offset_up.start()
+
+    @pl.when(has_prev)
+    def _():
+        rim_down(0).start()
+
     def one_hot(ref, values, depth):
         count = values.shape[1]
         spread = jnp.transpose(jnp.broadcast_to(values.astype(jnp.float32), (BLK, count)))
@@ -210,15 +225,16 @@
     hits = jnp.dot(
         jnp.ones((8, slots), jnp.bfloat16), pick_send[...], preferred_element_type=jnp.float32
     )
-    chosen = hits > 0.5
+    lane = lax.broadcasted_iota(jnp.int32, (8, stations), 1).astype(jnp.float32)
+    chosen = (hits > 0.5) & (lane >= float(chunk))
     mark = chosen.astype(jnp.float32)
     from_row = lax.broadcasted_iota(jnp.int32, (stations, stations), 0)
     to_lane = lax.broadcasted_iota(jnp.int32, (stations, stations), 1)
     up_to = (from_row <= to_lane).astype(jnp.float32).astype(jnp.bfloat16)
     running = jnp.dot(mark.astype(jnp.bfloat16), up_to, preferred_element_type=jnp.float32)
-    lane = lax.broadcasted_iota(jnp.int32, (8, stations), 1).astype(jnp.float32)
     total = jnp.sum(mark, axis=1, keepdims=True)
-    place = jnp.where(chosen, running - 1.0, total + lane - running)
+    place = jnp.where(chosen, float(chunk - 1) + running, total + lane - running)
+    place = jnp.where(lane < float(chunk), lane, place)
     order[...] = (
         (place[:1] == from_row.astype(jnp.float32)).astype(jnp.float32).astype(jnp.bfloat16)
     )
@@ -234,25 +250,19 @@
             order[rows], raw[:, columns], preferred_element_type=jnp.float32
         ).astype(jnp.bfloat16)
 
-    for c in range(CHUNKS + 1):
+    for c in [*range(1, CHUNKS + 1), 0]:
         arrange(rim_rows(c), slice(0, STEP))
         arrange(rim_rows(c), slice(TB - STEP, TB))
 
-        if c == 0:
-            greeted = n_sta - 1 + has_prev.astype(jnp.int32) + has_next.astype(jnp.int32)
-            pl.semaphore_wait(barrier, greeted)
+        if c > 0:
 
             @pl.when(has_next)
             def _():
-                offset_up.start()
-
-        @pl.when(has_next)
-        def _():
-            rim_up(c).start()
-
-        @pl.when(has_prev)
-        def _():
-            rim_down(c).start()
+                rim_up(c).start()
+
+            @pl.when(has_prev)
+            def _():
+                rim_down(c).start()
 
     load_middle.wait()
     arrange(slice(0, stations), slice(STEP, TB - STEP))
@@ -323,7 +333,7 @@
             )
         return result
 
-    lead = min(slots, stations)
+    lead = 2 * chunk if early else stations
 
     def start_swap(which, slot, depth):
         for w in range(slot, slot + depth):
@@ -446,11 +456,12 @@
             add_cross((3,), 0, stations)
 
     two_windows(0, 0, chunk)
+    finish_early_windows()
+    two_windows(1, chunk, chunk)
     if early:
         start_swap(1, 1, 2)
-    finish_early_windows()
-
-    @pl.loop(1, CHUNKS - 1)
+
+    @pl.loop(2, CHUNKS - 1)
     def _(c):
         two_windows(c, c * chunk, chunk)
 

time: 65.7 us -> 65.1 us (level)
  no operation moved by 1% of the time
where the time goes in v6:
time: 65.1 us; the launch traced here: 64.9 us
  Pallas kernels  63 us (97%)
  local copies, waits for them, and re-layouts  1.87 us (3%)
    pallas_call x1, Pallas kernels, on_device(): pl.pallas_call(functools.partial(kernel, n_tm, n_sta), out_shape=jax.Shap...  63 us
    unnamed x1, local copies, waits for them, and re-layouts  1.87 us

profile of v6, /device:TPU:0, one launch (start us, length us, event | category | flops | bytes accessed | tf_op | source)
XLA Modules:
  0.0 64.9 jit_solution(5588817273684972790)
XLA Ops:
  0.0 63.0 %shard_map.91 = f32[256,512]{1,0:T(8,128)} custom-call(s32[3]{0:T(128)} %offsets.1, s32[1,512]{1,0:T(1,128)} %bitcast.2, s32[1,512]{1,0:T(1,128)} %bitcast.3, s32[1,128]{1,0:T(1,128)} %send_rows.1, f32[1,2048]{1,0:T(1,128)} %constant.8.clone.taper, f32[1,1024]{1,0:T(1,128)} %constant.9.clone.rest, bf16[512,3072]{1,0:T(8,128)(2,1)} %traces.1, ...), custom_call_target="tpu_custom_call" | custom-call | tf_op jit(solution)/shard_map/pallas_call | solution.py:618
  63.0 1.9 %copy.11 = f32[256,512]{1,0:T(8,128)} copy(f32[256,512]{1,0:T(8,128)} %shard_map.91) | data formatting | bytes 1048576

commit v7 on v5

--- a/solution.py
+++ b/solution.py
@@ -18,7 +18,7 @@
 FAR_ROWS = 16
 FLOOR = 0.1
 CHUNKS = 4
-PIECES = 4
+PIECES = 2
 BLK = 128
 ROWS = 16
 MESH = pl.DeviceIdType.MESH
@@ -113,7 +113,6 @@
     lag_rows = out.shape[0]
     slots = n_sta * CAP
     chunk = stations // CHUNKS
-    half = chunk // 2
     early = slots <= chunk
     tm = lax.axis_index("tm")
     me = lax.axis_index("sta")
@@ -162,8 +161,6 @@
         pl.semaphore_signal(barrier, inc=1, device_id={"tm": tm + 1}, device_id_type=MESH)
 
     def rim_rows(c):
-        if isinstance(c, int) and c >= CHUNKS - 1:
-            return pl.ds((CHUNKS - 1) * chunk + (c - CHUNKS + 1) * half, half)
         return pl.ds(c * chunk, chunk)
 
     def rim_up(c):
@@ -234,7 +231,7 @@
             order[rows], raw[:, columns], preferred_element_type=jnp.float32
         ).astype(jnp.bfloat16)
 
-    for c in range(CHUNKS + 1):
+    for c in range(CHUNKS):
         arrange(rim_rows(c), slice(0, STEP))
         arrange(rim_rows(c), slice(TB - STEP, TB))
 
@@ -282,25 +279,51 @@
         )
         spec[...] = (first - means[:, :1] * rest[...]) * scale
 
-    def single_window(slot, jitter, blocks_at, half_window=False):
+    def whiten_group(slot, row):
+        re, im = whiten_rows(spec, row)
+        white[slot, pl.ds(row, ROWS), :NF] = re
+        white[slot, pl.ds(row, ROWS), NF:] = im
+
+    def whole_window(slot, jitter, blocks_at):
+        batch = stations // 2
+
+        @pl.loop(0, batch // ROWS, unroll=4)
+        def _(g):
+            row = pl.multiple_of(g * ROWS, ROWS)
+            write_segment(blocks_at(row), jitter, taper, seg, row)
+
+        width = 2 * NF // 4
+        share = batch // ROWS // 4
+        for b in range(2):
+            rows = slice(b * batch, (b + 1) * batch)
+            for j in range(4):
+                columns = slice(j * width, (j + 1) * width)
+                spec[rows, columns] = (
+                    jnp.dot(seg[rows], table[:, columns], preferred_element_type=jnp.float32)
+                    * scale
+                )
+                for g in range(j * share, (j + 1) * share):
+                    if b == 0:
+                        row = batch + g * ROWS
+                        write_segment(blocks_at(row), jitter, taper, seg, row)
+                    else:
+                        whiten_group(slot, g * ROWS)
+
+        @pl.loop(0, batch // ROWS, unroll=4)
+        def _(g):
+            whiten_group(slot, pl.multiple_of(batch + g * ROWS, ROWS))
+
+    def half_window(slot, jitter, blocks_at):
         @pl.loop(0, stations // ROWS, unroll=4)
         def _(g):
             row = pl.multiple_of(g * ROWS, ROWS)
-            write_segment(
-                blocks_at(row), jitter, taper, seg, row, means if half_window else None
-            )
-
-        if half_window:
-            transform_half()
-        else:
-            transform(stations)
+            write_segment(blocks_at(row), jitter, taper, seg, row, means)
+
+        transform_half()
 
         @pl.loop(0, stations // ROWS, unroll=4)
         def _(g):
-            row = pl.multiple_of(g * ROWS, ROWS)
-            re, im = whiten_rows(spec, row)
-            white[slot, pl.ds(row, ROWS), :NF] = re
-            white[slot, pl.ds(row, ROWS), NF:] = im
+            whiten_group(slot, pl.multiple_of(g * ROWS, ROWS))
 
     def swap(which, slot, depth):
         result = []
@@ -380,17 +403,16 @@
         def _(p):
             cross_part(p, windows, low, high, fresh=fresh)
 
-    single_window(0, offsets[0], lambda row: load_blocks(own, row, 0, 24))
+    whole_window(0, offsets[0], lambda row: load_blocks(own, row, 0, 24))
     start_swap(0, 0, 1)
 
     @pl.when(is_last)
     def _():
-        single_window(
+        half_window(
             3,
             offsets[2] - 2 * STEP,
             lambda row: load_blocks(own, row, 16, 8)
             + [jnp.zeros((ROWS, BLK), jnp.bfloat16)] * 8,
-            half_window=True,
         )
         start_swap(2, 3, 1)
 
@@ -458,8 +480,7 @@
     if early:
         end_swap(1, 1, 2)
         add_cross((1, 2), 0, last)
-    two_windows(CHUNKS - 1, last, half)
-    two_windows(CHUNKS, last + half, half)
+    two_windows(CHUNKS - 1, last, chunk)
     if not early:
         start_swap(1, 1, 2)
         end_swap(1, 1, 2)
@@ -570,7 +591,7 @@
     def _():
         offset_up.wait_send()
 
-    for c in range(CHUNKS + 1):
+    for c in range(CHUNKS):
 
         @pl.when(has_next)
         def _():
@@ -638,8 +659,8 @@
             pltpu.VMEM((8, BLK), jnp.int32),
             pltpu.VMEM((8, BLK), jnp.int32),
             dma((5,)),
-            dma((2, CHUNKS + 1)),
-            dma((2, CHUNKS + 1)),
+            dma((2, CHUNKS)),
+            dma((2, CHUNKS)),
             dma((2,)),
             dma((3, n_sta)),
             dma((3, n_sta)),

time: 65.7 us -> 60.1 us (0.915)
  Pallas kernels: 63.6 us -> 58 us
    pallas_call x1, Pallas kernels: 63.6 us -> 58 us  [on_device(): pl.pallas_call(functools.partial(kernel, n_tm, n_sta), out_shape=jax.Shap...]
where the time goes in v7:
time: 60.1 us; the launch traced here: 59.9 us
  Pallas kernels  58 us (97%)
  local copies, waits for them, and re-layouts  1.87 us (3%)
    pallas_call x1, Pallas kernels, on_device(): pl.pallas_call(functools.partial(kernel, n_tm, n_sta), out_shape=jax.Shap...  58 us
    unnamed x1, local copies, waits for them, and re-layouts  1.87 us

profile of v7, /device:TPU:0, one launch (start us, length us, event | category | flops | bytes accessed | tf_op | source)
XLA Modules:
  0.0 59.9 jit_solution(8285547827077771356)
XLA Ops:
  0.0 58.0 %shard_map.91 = f32[256,512]{1,0:T(8,128)} custom-call(s32[3]{0:T(128)} %offsets.1, s32[1,512]{1,0:T(1,128)} %bitcast.2, s32[1,512]{1,0:T(1,128)} %bitcast.3, s32[1,128]{1,0:T(1,128)} %send_rows.1, f32[1,2048]{1,0:T(1,128)} %constant.8.clone.taper, f32[1,1024]{1,0:T(1,128)} %constant.9.clone.rest, bf16[512,3072]{1,0:T(8,128)(2,1)} %traces.1, ...), custom_call_target="tpu_custom_call" | custom-call | tf_op jit(solution)/shard_map/pallas_call | solution.py:628
  58.0 1.9 %copy.11 = f32[256,512]{1,0:T(8,128)} copy(f32[256,512]{1,0:T(8,128)} %shard_map.91) | data formatting | bytes 1048576

commit v8 on v7

--- a/solution.py
+++ b/solution.py
@@ -433,7 +433,7 @@
         def _():
             rim_down(c).wait_recv()
 
-        @pl.loop(0, size // ROWS, unroll=2)
+        @pl.loop(0, size // ROWS, unroll=4)
         def _(g):
             row = pl.multiple_of(start + g * ROWS, ROWS)
             at = pl.multiple_of(g * ROWS, ROWS)
@@ -448,7 +448,7 @@
 
         transform(2 * size)
 
-        @pl.loop(0, size // ROWS, unroll=2)
+        @pl.loop(0, size // ROWS, unroll=4)
         def _(g):
             row = pl.multiple_of(start + g * ROWS, ROWS)
             re, im = whiten_rows(spec, pl.multiple_of(g * ROWS, ROWS))

time: 60.1 us -> 61.2 us (1.018)
  Pallas kernels: 58 us -> 59.1 us
    pallas_call x1, Pallas kernels: 58 us -> 59.1 us  [on_device(): pl.pallas_call(functools.partial(kernel, n_tm, n_sta), out_shape=jax.Shap...]
where the time goes in v8:
time: 61.2 us; the launch traced here: 60.9 us
  Pallas kernels  59.1 us (97%)
  local copies, waits for them, and re-layouts  1.87 us (3%)
    pallas_call x1, Pallas kernels, on_device(): pl.pallas_call(functools.partial(kernel, n_tm, n_sta), out_shape=jax.Shap...  59.1 us
    unnamed x1, local copies, waits for them, and re-layouts  1.87 us

profile of v8, /device:TPU:0, one launch (start us, length us, event | category | flops | bytes accessed | tf_op | source)
XLA Modules:
  0.0 60.9 jit_solution(5382588267131805758)
XLA Ops:
  0.0 59.1 %shard_map.91 = f32[256,512]{1,0:T(8,128)} custom-call(s32[3]{0:T(128)} %offsets.1, s32[1,512]{1,0:T(1,128)} %bitcast.2, s32[1,512]{1,0:T(1,128)} %bitcast.3, s32[1,128]{1,0:T(1,128)} %send_rows.1, f32[1,2048]{1,0:T(1,128)} %constant.8.clone.taper, f32[1,1024]{1,0:T(1,128)} %constant.9.clone.rest, bf16[512,3072]{1,0:T(8,128)(2,1)} %traces.1, ...), custom_call_target="tpu_custom_call" | custom-call | tf_op jit(solution)/shard_map/pallas_call | solution.py:628
  59.1 1.9 %copy.11 = f32[256,512]{1,0:T(8,128)} copy(f32[256,512]{1,0:T(8,128)} %shard_map.91) | data formatting | bytes 1048576
